TPU v7x, 128 devices: a whole 4x4x4 slice. The times are simulated.
128 devices in a mesh: col: 4 (over x_hi, core), af: 32 (over z, x_lo, y).
Axes of the slice: x: 4 (x_hi: 2, x_lo: 2; x = x_hi * 2 + x_lo), y: 4, z: 4, core: 2. Of those that a mesh axis runs over, the one named last changes fastest.
Arguments:
- coarse_state: float32 [3, 8, 512, 1024], P(None, None, 'af', 'col'), may hold values from 0.1 to 2
- coarse_kappa: float32 [8, 512, 1024], P(None, 'af', 'col'), may hold values from 0.25 to 1
- coarse_rate: float32 [8, 512, 1024], P(None, 'af', 'col'), may hold values from 0.5 to 6
- fine_state: float32 [512, 3, 32, 1024], P(('col', 'af')), may hold values from 0.1 to 2
- fine_kappa: float32 [512, 32, 1024], P(('col', 'af')), may hold values from 0.25 to 1
- fine_rate: float32 [512, 32, 1024], P(('col', 'af')), may hold values from 0.5 to 6
- boxes: int32 [512, 2], replicated, may hold values from 0 to 127, as said below
- cover: int32 [64, 128], replicated, may hold values from -1 to 511, as said below
Outputs:
- coarse_out: float32 [3, 8, 512, 1024], P(None, None, 'af', 'col')
- fine_out: float32 [512, 3, 32, 1024], P(('col', 'af'))
Inputs may be any that keep to these rules, and one draw needn't show every extreme that they name: `boxes`: A patch's block spans all 8 planes; it lies in the 32 block rows of one col index, never in the first or last of them nor in the slab's first or last block column, and no two patches share a face. The patches whose blocks lie in one col index's rows are the rows of the fine arrays held by that col index, in no particular order. The 2 block columns of one af index hold at most 10 patches, and in every col index some af index holds exactly that many. cover[bx, by] is the patch whose block is (bx, by), or -1 where none is; it agrees with boxes, and every patch appears once.
All inputs are finite; a program needn't handle non-finite values.
Results may differ from a plain program's by a relative error of at most 0.0003.
Values sent between devices are 32-bit elements; how exact they have to be, the bound alone decides.
A program may use at most 192 MiB of HBM per device.

v0:
```python
import jax
import jax.numpy as jnp
from jax import lax
from jax.sharding import PartitionSpec as P

NZC = 8
RATIO = 4
BLK = 8


DT_COARSE = 1.0 / 28.0
DIFFUSE = (1.0, 0.7, 0.45)
NEIGHBOURS = ((1, 0, 0), (-1, 0, 0), (0, 1, 0), (0, -1, 0), (0, 0, 1), (0, 0, -1))


def with_halo(cells, sides, width):
    for axis, dim in sides:
        count = lax.axis_size(axis)
        ends = count - 1
        head = lax.slice_in_dim(cells, 0, width, axis=dim)
        tail = lax.slice_in_dim(cells, cells.shape[dim] - width, cells.shape[dim], axis=dim)
        cells = jnp.concatenate(
            [
                lax.ppermute(tail, axis, [(i, (i + 1) % count) for i in range(ends)]),
                cells,
                lax.ppermute(head, axis, [((i + 1) % count, i) for i in range(ends)]),
            ],
            axis=dim,
        )
    return cells


def harmonic(first, second):
    summed = first + second
    positive = summed > 0.0
    return jnp.where(positive, 2.0 * first * second / jnp.where(positive, summed, 1.0), 0.0)


def combine(center, conduct, neighbour_list, reaction, inv_square, step_size):
    summed = jnp.zeros_like(center)
    for values, coeffs in neighbour_list:
        summed = summed + harmonic(conduct, coeffs) * (values - center)
    spread = (
        jnp.stack([DIFFUSE[0] * summed[0], DIFFUSE[1] * summed[1], DIFFUSE[2] * summed[2]])
        * inv_square
    )
    forward = reaction * (center[0] * center[1] - center[2])
    change = spread + jnp.stack([-forward, -forward, forward])
    return center + step_size * change


def window(values, step_z, step_x, step_y):
    depth_len = values.shape[-3] - 2
    across = values.shape[-2] - 2
    along_len = values.shape[-1] - 2
    return values[
        ...,
        1 + step_z : 1 + step_z + depth_len,
        1 + step_x : 1 + step_x + across,
        1 + step_y : 1 + step_y + along_len,
    ]


def coarse_advance(padded_xy, conduct_xy, reaction):
    padded = jnp.pad(padded_xy, ((0, 0), (1, 1), (0, 0), (0, 0)))
    conduct = jnp.pad(conduct_xy, ((1, 1), (0, 0), (0, 0)))
    neighbour_list = [
        (
            window(padded, offsets[0], offsets[1], offsets[2]),
            window(conduct, offsets[0], offsets[1], offsets[2]),
        )
        for offsets in NEIGHBOURS
    ]
    return combine(
        window(padded, 0, 0, 0), window(conduct, 0, 0, 0), neighbour_list, reaction, 1.0, DT_COARSE
    )


def upsample(strips):
    return jnp.repeat(jnp.repeat(strips, RATIO, axis=-2), RATIO, axis=-1)


def patch_step(fields, conduct, reaction, strips):
    ghosts = upsample(strips)
    edge_len = ghosts.shape[-1]
    position = lax.broadcasted_iota(jnp.int32, (1, edge_len * edge_len), 1)
    column = position % edge_len
    row_pos = position // edge_len
    zero_fields = jnp.zeros_like(fields[:, :1])
    zero_conduct = jnp.zeros_like(conduct[:1])
    upward = (
        jnp.concatenate([fields[:, 1:], zero_fields], axis=1),
        jnp.concatenate([conduct[1:], zero_conduct], axis=0),
    )
    downward = (
        jnp.concatenate([zero_fields, fields[:, :-1]], axis=1),
        jnp.concatenate([zero_conduct, conduct[:-1]], axis=0),
    )
    last_row = row_pos == edge_len - 1
    first_row = row_pos == 0
    last_col = column == edge_len - 1
    first_col = column == 0
    next_x = (
        jnp.where(
            last_row, jnp.tile(ghosts[1], (1, 1, edge_len)), jnp.roll(fields, -edge_len, axis=-1)
        ),
        jnp.where(last_row, conduct, jnp.roll(conduct, -edge_len, axis=-1)),
    )
    prev_x = (
        jnp.where(
            first_row, jnp.tile(ghosts[0], (1, 1, edge_len)), jnp.roll(fields, edge_len, axis=-1)
        ),
        jnp.where(first_row, conduct, jnp.roll(conduct, edge_len, axis=-1)),
    )
    next_y = (
        jnp.where(
            last_col, jnp.repeat(ghosts[3], edge_len, axis=-1), jnp.roll(fields, -1, axis=-1)
        ),
        jnp.where(last_col, conduct, jnp.roll(conduct, -1, axis=-1)),
    )
    prev_y = (
        jnp.where(
            first_col, jnp.repeat(ghosts[2], edge_len, axis=-1), jnp.roll(fields, 1, axis=-1)
        ),
        jnp.where(first_col, conduct, jnp.roll(conduct, 1, axis=-1)),
    )
    return combine(
        fields,
        conduct,
        [upward, downward, next_x, prev_x, next_y, prev_y],
        reaction,
        float(RATIO * RATIO),
        DT_COARSE / RATIO,
    )


def restrict(fields):
    shaped = fields.reshape(3, NZC, RATIO, BLK, RATIO, BLK, RATIO)
    return jnp.mean(shaped, axis=(2, 4, 6)).reshape(-1)


def rim_rows(outer, block_cols, block_rows):
    species, planes, reach_x, cells_y = outer.shape
    padded_y = jnp.pad(outer, ((0, 0), (0, 0), (0, 0), (1, 1)))
    collected = []
    for column in range(block_cols):
        base_x = BLK * column
        lower_x = (
            outer[:, :, base_x, :].reshape(species, planes, block_rows, BLK).transpose(2, 0, 1, 3)
        )
        upper_x = (
            outer[:, :, base_x + BLK + 1, :]
            .reshape(species, planes, block_rows, BLK)
            .transpose(2, 0, 1, 3)
        )
        lower_y = padded_y[:, :, base_x + 1 : base_x + 1 + BLK, 0:cells_y:BLK].transpose(3, 0, 1, 2)
        upper_y = padded_y[
            :, :, base_x + 1 : base_x + 1 + BLK, BLK + 1 : cells_y + 2 : BLK
        ].transpose(3, 0, 1, 2)
        face_rows = jnp.stack([lower_x, upper_x, lower_y, upper_y], axis=1)
        collected.append(face_rows.reshape(block_rows, -1))
    return jnp.concatenate(collected, axis=0)


def sum_sources(received):
    return jnp.sum(received, axis=0)


def per_device(
    coarse_state, coarse_kappa, coarse_rate, fine_state, fine_kappa, fine_rate, boxes, cover
):
    af_count = lax.axis_size("af")
    af_index = lax.axis_index("af")
    col_index = lax.axis_index("col")
    slot_count = fine_state.shape[0]
    cells_x = coarse_state.shape[2]
    cells_y = coarse_state.shape[3]
    block_cols = cells_x // BLK
    block_rows = cells_y // BLK
    group_size = af_count * slot_count
    group_base = col_index * group_size
    stacked = jnp.concatenate([coarse_state, coarse_kappa[None]], axis=0)
    widened = with_halo(stacked, (("col", 3), ("af", 2)), 1)
    coarse_new = coarse_advance(widened[:3], widened[3], coarse_rate)
    outer_new = with_halo(coarse_new, (("af", 2),), 1)
    outer_old = widened[:3, :, :, 1:-1]
    group_boxes = lax.dynamic_slice_in_dim(boxes, group_base, group_size, 0)
    local_x = group_boxes[:, 0] - af_index * block_cols
    local_y = group_boxes[:, 1] - col_index * block_rows
    inside = (local_x >= 0) & (local_x < block_cols) & (local_y >= 0) & (local_y < block_rows)
    block_ids = jnp.where(inside, local_x * block_rows + local_y, -1)
    targets = (
        block_ids[:, None] == jnp.arange(block_cols * block_rows, dtype=jnp.int32)[None, :]
    ).astype(jnp.float32)
    earlier = rim_rows(outer_old, block_cols, block_rows)
    updated = rim_rows(outer_new, block_cols, block_rows)
    fields = fine_state
    for substep in range(RATIO):
        fraction = substep / RATIO
        current = earlier + fraction * (updated - earlier)
        send_rows = jnp.dot(targets, current, precision=lax.Precision.HIGHEST)
        strips = sum_sources(
            lax.all_to_all(
                send_rows.reshape(af_count, slot_count, current.shape[1]),
                "af",
                split_axis=0,
                concat_axis=0,
                tiled=True,
            )
        )
        strips = strips.reshape(slot_count, 4, 3, NZC, BLK)
        fields = jax.vmap(patch_step)(fields, fine_kappa, fine_rate, strips)
    averages = jax.vmap(restrict)(fields)
    cover_mine = lax.dynamic_slice(
        cover, (af_index * block_cols, col_index * block_rows), (block_cols, block_rows)
    ).reshape(-1)
    wanted = cover_mine - group_base
    portion = lax.all_gather(averages, "af", axis=0, tiled=True)
    selector = (wanted[:, None] == jnp.arange(portion.shape[0], dtype=jnp.int32)[None, :]).astype(
        jnp.float32
    )
    placed = jnp.dot(selector, portion, precision=lax.Precision.HIGHEST)
    placed = (
        placed.reshape(block_cols, block_rows, 3, NZC, BLK, BLK)
        .transpose(2, 3, 0, 4, 1, 5)
        .reshape(3, NZC, cells_x, cells_y)
    )
    covered = (cover_mine >= 0).reshape(block_cols, block_rows)
    covered = jnp.repeat(jnp.repeat(covered, BLK, axis=0), BLK, axis=1)
    coarse_out = jnp.where(covered[None, None], placed, coarse_new)
    return (coarse_out, fields)


def solution(mesh):
    return jax.shard_map(
        per_device,
        mesh=mesh,
        in_specs=(
            P(None, None, "af", "col"),
            P(None, "af", "col"),
            P(None, "af", "col"),
            P(("col", "af"), None, None, None),
            P(("col", "af"), None, None),
            P(("col", "af"), None, None),
            P(),
            P(),
        ),
        out_specs=(P(None, None, "af", "col"), P(("col", "af"), None, None, None)),
        check_vma=False,
    )
```

profile of v0, /device:TPU:4, one launch (start us, length us, event | category | flops | bytes accessed | tf_op | source)
XLA Modules:
  0.0 597.3 jit_solution(5692772814283135084)
XLA Ops:
  4.6 5.1 collective-permute-start.1
  31.8 4.5 compare_select_fusion.10
  124.3 12.2 %all-to-all-start = ((f32[32,4,768]{2,1,0:T(4,128)}), f32[32,4,768]{2,1,0:T(4,128)}, u32[]{:S(2)}, u32[]{:S(2)}) async-start(f32[32,4,768]{2,1,0:T(4,128)} %reshape.321), calls=%async_computation | async-start | bytes 786432 | tf_op jit(solution)/shard_map/all_to_all | solution.py:203
  146.5 8.9 %all-to-all-start.1 = ((f32[32,4,768]{2,1,0:T(4,128)}), f32[32,4,768]{2,1,0:T(4,128)}, u32[]{:S(2)}, u32[]{:S(2)}) async-start(f32[32,4,768]{2,1,0:T(4,128)} %reshape.327), calls=%async_computation.1 | async-start | bytes 786432 | tf_op jit(solution)/shard_map/all_to_all | solution.py:203
  166.0 5.9 reshape.325
  175.8 5.9 reshape.326
  184.8 5.9 tile.82
  193.8 6.0 %tile.85 = f32[4,3,32,1024]{3,2,0,1:T(8,128)} reshape(f32[4,3,32,32,32]{4,3,2,0,1:T(8,128)} %tile.84) | data formatting | bytes 3145728 | tf_op jit(solution)/shard_map/vmap()/tile | solution.py:111
  199.8 7.7 %fusion.5 = f32[4,3,32,1024]{3,2,0,1:T(8,128)S(1)} fusion(f32[4,3,32,1024]{3,2,0,1:T(8,128)} %tile.82, f32[4,3,32,32]{3,2,0,1:T(8,128)} %get-tuple-element.69, f32[4,3,32,992]{3,2,0,1:T(8,128)} %get-tuple-element.71, f32[4,3,32,1024]{3,2,0,1:T(8,128)} %tile.85, f32[4,3,32,992]{3,2,0,1:T(8,128)} %get-tuple-element.70, f32[4,3,32,32]{3,2,0,1:T(8,128)} %get-tuple-element.68, ...), kind=kLoop, calls=%fused_computation.8 | loop fusion | flops 9830400 | bytes 21925888 | tf_op jit(solution)/shard_map/vmap()/add | solution.py:42
  218.0 8.4 %all-to-all-start.2 = ((f32[32,4,768]{2,1,0:T(4,128)}), f32[32,4,768]{2,1,0:T(4,128)S(1)}, u32[]{:S(2)}, u32[]{:S(2)}) async-start(f32[32,4,768]{2,1,0:T(4,128)} %reshape.333), calls=%async_computation.2 | async-start | bytes 786432 | tf_op jit(solution)/shard_map/all_to_all | solution.py:203
  236.2 4.8 broadcast_in_dim.335
  241.0 5.9 reshape.331
  248.6 4.8 broadcast_in_dim.336
  253.4 5.9 reshape.332
  265.0 5.9 tile.88
  276.5 5.9 tile.91
  282.5 8.4 %fusion.21 = f32[4,3,32,1024]{3,2,0,1:T(8,128)S(1)} fusion(f32[4,3,32,1024]{3,2,0,1:T(8,128)} %tile.88, f32[4,3,32,32]{3,2,0,1:T(8,128)} %get-tuple-element.56, f32[4,3,32,992]{3,2,0,1:T(8,128)} %get-tuple-element.58, f32[4,3,32,1024]{3,2,0,1:T(8,128)} %tile.91, f32[4,3,32,992]{3,2,0,1:T(8,128)} %get-tuple-element.57, ...), kind=kLoop, calls=%fused_computation.29 | loop fusion | flops 12976128 | bytes 24547328 | tf_op jit(solution)/shard_map/vmap()/add | solution.py:42
  303.2 8.6 %all-to-all-start.3 = ((f32[32,4,768]{2,1,0:T(4,128)}), f32[32,4,768]{2,1,0:T(4,128)}, u32[]{:S(2)}, u32[]{:S(2)}) async-start(f32[32,4,768]{2,1,0:T(4,128)} %reshape.339), calls=%async_computation.3 | async-start | bytes 786432 | tf_op jit(solution)/shard_map/all_to_all | solution.py:203
  320.4 5.9 reshape.337
  331.0 5.9 reshape.338
  341.0 5.9 tile.94
  350.0 6.0 %tile.97 = f32[4,3,32,1024]{3,2,0,1:T(8,128)} reshape(f32[4,3,32,32,32]{4,3,2,0,1:T(8,128)} %tile.96) | data formatting | bytes 3145728 | tf_op jit(solution)/shard_map/vmap()/tile | solution.py:111
  356.1 10.2 %fusion.37 = f32[4,3,32,1024]{3,2,0,1:T(8,128)S(1)} fusion(f32[4,3,32,1024]{3,2,0,1:T(8,128)} %tile.94, f32[4,3,32,32]{3,2,0,1:T(8,128)} %get-tuple-element.43, f32[4,3,32,992]{3,2,0,1:T(8,128)} %get-tuple-element.45, f32[4,3,32,1024]{3,2,0,1:T(8,128)} %tile.97, f32[4,3,32,992]{3,2,0,1:T(8,128)} %get-tuple-element.44, ...), kind=kLoop, calls=%fused_computation.50 | loop fusion | flops 16121856 | bytes 27168768 | tf_op jit(solution)/shard_map/vmap()/add | solution.py:42
  384.3 5.9 reshape.343
  394.1 5.9 reshape.344
  403.1 5.9 tile.100
  412.1 6.1 %tile.103 = f32[4,3,32,1024]{3,2,0,1:T(8,128)} reshape(f32[4,3,32,32,32]{4,3,2,0,1:T(8,128)} %tile.102) | data formatting | bytes 3145728 | tf_op jit(solution)/shard_map/vmap()/tile | solution.py:111
  418.2 7.3 %fusion.50 = f32[4,3,32,1024]{3,2,0,1:T(8,128)S(1)} fusion(f32[4,3,32,1024]{3,2,0,1:T(8,128)} %tile.100, f32[4,3,32,1024]{3,2,0,1:T(8,128)} %tile.103, f32[4,3,32,1024]{3,2,0,1:T(8,128)} %reshape.343, f32[4,3,32,1024]{3,2,0,1:T(8,128)} %reshape.344, f32[4,32,1024]{2,1,0:T(8,128)} %get-tuple-element.95, f32[4,32,1024]{2,1,0:T(8,128)S(1)} %copy-done.21, ...), kind=kLoop, calls=%fused_computation.68 | loop fusion | flops 9830400 | bytes 21925888 | tf_op jit(solution)/shard_map/vmap()/add | solution.py:42
  427.1 53.4 %reshape.345 = f32[4,3,8,4,8,4,8,4]{7,6,5,4,3,2,1,0:T(8,128)} reshape(f32[4,3,32,1024]{3,2,1,0:T(8,128)S(1)} %bitcast_add_fusion) | data formatting | bytes 3145728 | tf_op jit(solution)/shard_map/vmap()/reshape | solution.py:138
  480.5 17.8 %reduce_sum.49 = f32[4,3,8,8,8]{4,3,2,1,0:T(8,128)S(1)} reduce(f32[4,3,8,4,8,4,8,4]{7,6,5,4,3,2,1,0:T(8,128)} %reshape.345, f32[]{:T(128)} %constant.94.clone.1), dimensions={3,5,7}, to_apply=%region_4.5 | reduce | flops 387072 | bytes 1597444 | tf_op jit(solution)/shard_map/vmap()/reduce_sum | solution.py:139
  498.6 85.9 %all-gather = f32[32,4,1536]{2,1,0:T(4,128)S(1)} all-gather(f32[1,4,1536]{2,1,0:T(4,128)S(1)} %reshape.348), channel_id=1, replica_groups=mesh['col'=4,'af'=32] {'af'}, dimensions={0}, use_global_device_ids=true | all-gather | bytes 811008 | tf_op jit(solution)/shard_map/all_gather | solution.py:218
  590.5 5.7 reshape.347
  (371 shorter events, 246.7 us)
Async XLA Ops:
  0.6 25.3 %copy-start = (s32[512,2]{0,1:T(2,128)S(1)}, s32[512,2]{0,1:T(2,128)}, u32[]{:S(2)}) copy-start(s32[512,2]{0,1:T(2,128)} %param.14) | copy-start | bytes 12292
  0.6 11.4 %copy-start.3 = (f32[4,32,1024]{2,1,0:T(8,128)S(1)}, f32[4,32,1024]{2,1,0:T(8,128)}, u32[]{:S(2)}) copy-start(f32[4,32,1024]{2,1,0:T(8,128)} %param.12) | copy-start | bytes 1572868
  2.6 41.3 %collective-permute-start = (f32[4,8,16,1]{3,2,1,0:T(8,128)}, f32[4,8,16,1]{3,2,1,0:T(8,128)}, u32[]{:S(2)}, u32[]{:S(2)}) collective-permute-start(f32[4,8,16,1]{3,2,1,0:T(8,128)} %get-tuple-element.108), channel_id=1, source_target_pairs={{0,32},{32,64},{64,96},{1,33},{33,65},{65,97},{2,34},{34,66},{66,9... | collective-permute-start | bytes 6152 | tf_op jit(solution)/shard_map/ppermute | solution.py:24
  4.6 39.4 %collective-permute-start.1 = (f32[4,8,16,1]{3,2,1,0:T(8,128)}, f32[4,8,16,1]{3,2,1,0:T(8,128)}, u32[]{:S(2)}, u32[]{:S(2)}) collective-permute-start(f32[4,8,16,1]{3,2,1,0:T(8,128)} %get-tuple-element.109), channel_id=1, source_target_pairs={{32,0},{64,32},{96,64},{33,1},{65,33},{97,65},{34,2},{66,34},{98,6... | collective-permute-start | bytes 6152 | tf_op jit(solution)/shard_map/ppermute | solution.py:26
  11.5 188.3 %copy-start.72 = (pred[1024]{0:T(1024)(128)(4,1)}, pred[1024]{0:T(1024)(128)(4,1)S(1)}, u32[]{:S(2)}) copy-start(pred[1024]{0:T(1024)(128)(4,1)S(1)} %get-tuple-element.121) | copy-start | bytes 3076
  11.5 188.3 %copy-start.75 = (pred[1024]{0:T(1024)(128)(4,1)}, pred[1024]{0:T(1024)(128)(4,1)S(1)}, u32[]{:S(2)}) copy-start(pred[1024]{0:T(1024)(128)(4,1)S(1)} %get-tuple-element.122) | copy-start | bytes 3076
  12.1 187.7 %copy-start.78 = (pred[1024]{0:T(1024)(128)(4,1)}, pred[1024]{0:T(1024)(128)(4,1)S(1)}, u32[]{:S(2)}) copy-start(pred[1024]{0:T(1024)(128)(4,1)S(1)} %get-tuple-element.123) | copy-start | bytes 3076
  27.8 328.2 %copy-start.6 = (f32[1,4,32,1024]{3,2,1,0:T(8,128)}, f32[1,4,32,1024]{3,2,1,0:T(8,128)S(1)}, u32[]{:S(2)}) copy-start(f32[1,4,32,1024]{3,2,1,0:T(8,128)S(1)} %get-tuple-element.16) | copy-start | bytes 1572868
  27.8 328.2 %copy-start.8 = (f32[4,32,1024]{2,1,0:T(8,128)}, f32[4,32,1024]{2,1,0:T(8,128)S(1)}, u32[]{:S(2)}) copy-start(f32[4,32,1024]{2,1,0:T(8,128)S(1)} %get-tuple-element.17) | copy-start | bytes 1572868
  46.5 7.0 %collective-permute-start.2 = (f32[4,8,1,258]{3,1,2,0:T(8,128)S(1)}, f32[4,8,1,258]{3,1,2,0:T(8,128)S(1)}, u32[]{:S(2)}, u32[]{:S(2)}) collective-permute-start(f32[4,8,1,258]{3,1,2,0:T(8,128)S(1)} %get-tuple-element.89), channel_id=1, source_target_pairs={{0,1},{1,2},{2,3},{3,4},{4,5},{5,6},{6,7},{7,8},{8,9},{9,10},{10,1... | collective-permute-start | bytes 99080 | tf_op jit(solution)/shard_map/ppermute | solution.py:24
  50.0 6.0 %collective-permute-start.3 = (f32[4,8,1,258]{3,1,2,0:T(8,128)S(1)}, f32[4,8,1,258]{3,1,2,0:T(8,128)S(1)}, u32[]{:S(2)}, u32[]{:S(2)}) collective-permute-start(f32[4,8,1,258]{3,1,2,0:T(8,128)S(1)} %get-tuple-element.88), channel_id=1, source_target_pairs={{1,0},{2,1},{3,2},{4,3},{5,4},{6,5},{7,6},{8,7},{9,8},{10,9},{11,1... | collective-permute-start | bytes 99080 | tf_op jit(solution)/shard_map/ppermute | solution.py:26
  74.1 9.4 %copy-start.63 = (f32[3,8,8,32]{3,1,2,0:T(8,128)S(1)}, f32[3,8,8,32]{3,1,2,0:T(8,128)}, u32[]{:S(2)}) copy-start(f32[3,8,8,32]{3,1,2,0:T(8,128)} %slice.500) | copy-start | bytes 73732
  74.2 10.0 %copy-start.48 = (f32[1,8,16,256]{3,2,1,0:T(8,128)}, f32[1,8,16,256]{3,2,1,0:T(8,128)S(1)}, u32[]{:S(2)}) copy-start(f32[1,8,16,256]{3,2,1,0:T(8,128)S(1)} %copy.242) | copy-start | bytes 393220
  74.3 9.9 %copy-start.50 = (f32[1,8,16,256]{3,2,1,0:T(8,128)}, f32[1,8,16,256]{3,2,1,0:T(8,128)S(1)}, u32[]{:S(2)}) copy-start(f32[1,8,16,256]{3,2,1,0:T(8,128)S(1)} %copy.243) | copy-start | bytes 393220
  74.4 9.9 %copy-start.52 = (f32[1,8,16,256]{3,2,1,0:T(8,128)}, f32[1,8,16,256]{3,2,1,0:T(8,128)S(1)}, u32[]{:S(2)}) copy-start(f32[1,8,16,256]{3,2,1,0:T(8,128)S(1)} %copy.244) | copy-start | bytes 393220
  75.1 11.8 %copy-start.62 = (f32[3,8,8,32]{3,1,2,0:T(8,128)S(1)}, f32[3,8,8,32]{3,1,2,0:T(8,128)}, u32[]{:S(2)}) copy-start(f32[3,8,8,32]{3,1,2,0:T(8,128)} %slice.504) | copy-start | bytes 73732
  75.9 11.6 %copy-start.67 = (f32[4,8,1,258]{3,1,2,0:T(8,128)S(1)}, f32[4,8,1,258]{3,1,2,0:T(8,128)}, u32[]{:S(2)}) copy-start(f32[4,8,1,258]{3,1,2,0:T(8,128)} %copy-done.65) | copy-start | bytes 99076
  77.2 20.3 %collective-permute-start.4 = (f32[3,8,1,256]{3,1,2,0:T(8,128)}, f32[3,8,1,256]{3,1,2,0:T(8,128)}, u32[]{:S(2)}, u32[]{:S(2)}) collective-permute-start(f32[3,8,1,256]{3,1,2,0:T(8,128)} %copy.245), channel_id=1, source_target_pairs={{0,1},{1,2},{2,3},{3,4},{4,5},{5,6},{6,7},{7,8},{8,9},{9,10},{10,1... | collective-permute-start | bytes 73736 | tf_op jit(solution)/shard_map/ppermute | solution.py:24
  81.9 15.6 %collective-permute-start.5 = (f32[3,8,1,256]{3,1,2,0:T(8,128)}, f32[3,8,1,256]{3,1,2,0:T(8,128)}, u32[]{:S(2)}, u32[]{:S(2)}) collective-permute-start(f32[3,8,1,256]{3,1,2,0:T(8,128)} %copy.246), channel_id=1, source_target_pairs={{1,0},{2,1},{3,2},{4,3},{5,4},{6,5},{7,6},{8,7},{9,8},{10,9},{11,1... | collective-permute-start | bytes 73736 | tf_op jit(solution)/shard_map/ppermute | solution.py:26
  124.3 22.2 %all-to-all-start = ((f32[32,4,768]{2,1,0:T(4,128)}), f32[32,4,768]{2,1,0:T(4,128)}, u32[]{:S(2)}, u32[]{:S(2)}) async-start(f32[32,4,768]{2,1,0:T(4,128)} %reshape.321), calls=%async_computation | async-start | bytes 786432 | tf_op jit(solution)/shard_map/all_to_all | solution.py:203
  146.5 71.5 %all-to-all-start.1 = ((f32[32,4,768]{2,1,0:T(4,128)}), f32[32,4,768]{2,1,0:T(4,128)}, u32[]{:S(2)}, u32[]{:S(2)}) async-start(f32[32,4,768]{2,1,0:T(4,128)} %reshape.327), calls=%async_computation.1 | async-start | bytes 786432 | tf_op jit(solution)/shard_map/all_to_all | solution.py:203
  207.7 148.3 %copy-start.10 = (f32[1,4,32,1024]{3,2,1,0:T(8,128)}, f32[1,4,32,1024]{3,2,1,0:T(8,128)S(1)}, u32[]{:S(2)}) copy-start(f32[1,4,32,1024]{3,2,1,0:T(8,128)S(1)} %get-tuple-element.59) | copy-start | bytes 1572868
  218.0 85.2 %all-to-all-start.2 = ((f32[32,4,768]{2,1,0:T(4,128)}), f32[32,4,768]{2,1,0:T(4,128)S(1)}, u32[]{:S(2)}, u32[]{:S(2)}) async-start(f32[32,4,768]{2,1,0:T(4,128)} %reshape.333), calls=%async_computation.2 | async-start | bytes 786432 | tf_op jit(solution)/shard_map/all_to_all | solution.py:203
  303.2 75.3 %all-to-all-start.3 = ((f32[32,4,768]{2,1,0:T(4,128)}), f32[32,4,768]{2,1,0:T(4,128)}, u32[]{:S(2)}, u32[]{:S(2)}) async-start(f32[32,4,768]{2,1,0:T(4,128)} %reshape.339), calls=%async_computation.3 | async-start | bytes 786432 | tf_op jit(solution)/shard_map/all_to_all | solution.py:203
  356.1 10.5 %copy-start.29 = (f32[4,32,1024]{2,1,0:T(8,128)S(1)}, f32[4,32,1024]{2,1,0:T(8,128)}, u32[]{:S(2)}) copy-start(f32[4,32,1024]{2,1,0:T(8,128)} %get-tuple-element.15) | copy-start | bytes 1572868
  356.1 10.5 %copy-start.31 = (f32[1,4,32,1024]{3,2,1,0:T(8,128)S(1)}, f32[1,4,32,1024]{3,2,1,0:T(8,128)}, u32[]{:S(2)}) copy-start(f32[1,4,32,1024]{3,2,1,0:T(8,128)} %copy-done.30) | copy-start | bytes 1572868
  356.1 10.5 %copy-start.33 = (f32[1,4,32,1024]{3,2,1,0:T(8,128)S(1)}, f32[1,4,32,1024]{3,2,1,0:T(8,128)}, u32[]{:S(2)}) copy-start(f32[1,4,32,1024]{3,2,1,0:T(8,128)} %copy-done.32) | copy-start | bytes 1572868
  356.1 10.5 %copy-start.35 = (f32[1,4,32,1024]{3,2,1,0:T(8,128)S(1)}, f32[1,4,32,1024]{3,2,1,0:T(8,128)}, u32[]{:S(2)}) copy-start(f32[1,4,32,1024]{3,2,1,0:T(8,128)} %copy-done.34) | copy-start | bytes 1572868
  356.1 10.5 %copy-start.42 = (f32[1,4,32,1024]{3,2,1,0:T(8,128)S(1)}, f32[1,4,32,1024]{3,2,1,0:T(8,128)}, u32[]{:S(2)}) copy-start(f32[1,4,32,1024]{3,2,1,0:T(8,128)} %get-tuple-element.12) | copy-start | bytes 1572868
  356.1 10.5 %copy-start.43 = (f32[4,32,1024]{2,1,0:T(8,128)S(1)}, f32[4,32,1024]{2,1,0:T(8,128)}, u32[]{:S(2)}) copy-start(f32[4,32,1024]{2,1,0:T(8,128)} %get-tuple-element.13) | copy-start | bytes 1572868
  427.1 53.4 %copy-start.36 = (f32[4,3,32,1024]{3,2,1,0:T(8,128)}, f32[4,3,32,1024]{3,2,1,0:T(8,128)S(1)}, u32[]{:S(2)}) copy-start(f32[4,3,32,1024]{3,2,1,0:T(8,128)S(1)} %bitcast_add_fusion) | copy-start | bytes 4718596
  498.4 86.4 %copy-start.86 = (s32[64]{0:T(128)S(1)}, s32[64]{0:T(128)}, u32[]{:S(2)}) copy-start(s32[64]{0:T(128)} %sub.185) | copy-start | bytes 772
  (65 other events, 237.0 us)
where the time goes:
time: 608 us; the launch traced here: 597 us
  local copies, waits for them, and re-layouts  357 us (59%)
  other arithmetic  87.3 us (14%)
  blocking collectives  85.9 us (14%)
  starting transfers between devices  55.6 us (9%)
  matrix products  7.74 us (1%)
    all_gather x1, blocking collectives, per_device(): portion = lax.all_gather(averages, 'af', axis=0, tiled=True)  85.9 us
    reshape x1, local copies, waits for them, and re-layouts, restrict(): shaped = fields.reshape(3, NZC, RATIO, BLK, RATIO, BLK, RATIO)  53.4 us
    another operation x12, local copies, waits for them, and re-layouts, patch_step(): jnp.tile(ghosts[1], (1, 1, edge_len))  39.5 us
    another operation x12, local copies, waits for them, and re-layouts, patch_step(): jnp.tile(ghosts[0], (1, 1, edge_len))  38.9 us
    all_to_all x4, starting transfers between devices, per_device(): lax.all_to_all(send_rows.reshape(af_count, slot_count, current.shape[1]),...  38.1 us
    add x5, other arithmetic, combine(): summed = summed + harmonic(conduct, coeffs) * (values - center)  35.9 us
    reshape x4, local copies, waits for them, and re-layouts, patch_step(): jnp.repeat(ghosts[2], edge_len, axis=-1)  23.6 us
    reshape x4, local copies, waits for them, and re-layouts, patch_step(): jnp.repeat(ghosts[3], edge_len, axis=-1)  23.6 us
  transfers between devices with their start and end apart: 10, of which 1 were waited for; matrix products, arithmetic and copies ran while one was open for 44% of the time, Pallas kernels for 0%

commit v1 on v0

--- a/solution.py
+++ b/solution.py
@@ -1,11 +1,19 @@
 import jax
 import jax.numpy as jnp
 from jax import lax
+from jax.experimental import pallas as pl
+from jax.experimental.pallas import tpu as pltpu
 from jax.sharding import PartitionSpec as P
 
 NZC = 8
 RATIO = 4
 BLK = 8
+SLOT_DEV = 4
+FZ = 32
+FXY = 1024
+TILES = FXY // 128
+FINE_DT = 1.0 / 112.0
+FINE_SCALE = 16.0 / 112.0
 
 
 DT_COARSE = 1.0 / 28.0
@@ -76,67 +84,213 @@
     )
 
 
-def upsample(strips):
-    return jnp.repeat(jnp.repeat(strips, RATIO, axis=-2), RATIO, axis=-1)
-
-
-def patch_step(fields, conduct, reaction, strips):
-    ghosts = upsample(strips)
-    edge_len = ghosts.shape[-1]
-    position = lax.broadcasted_iota(jnp.int32, (1, edge_len * edge_len), 1)
-    column = position % edge_len
-    row_pos = position // edge_len
-    zero_fields = jnp.zeros_like(fields[:, :1])
-    zero_conduct = jnp.zeros_like(conduct[:1])
-    upward = (
-        jnp.concatenate([fields[:, 1:], zero_fields], axis=1),
-        jnp.concatenate([conduct[1:], zero_conduct], axis=0),
-    )
-    downward = (
-        jnp.concatenate([zero_fields, fields[:, :-1]], axis=1),
-        jnp.concatenate([zero_conduct, conduct[:-1]], axis=0),
-    )
-    last_row = row_pos == edge_len - 1
-    first_row = row_pos == 0
-    last_col = column == edge_len - 1
-    first_col = column == 0
-    next_x = (
-        jnp.where(
-            last_row, jnp.tile(ghosts[1], (1, 1, edge_len)), jnp.roll(fields, -edge_len, axis=-1)
+def lanes(shape=(8, 128)):
+    return lax.broadcasted_iota(jnp.int32, shape, 1)
+
+
+def rot(x, shift):
+    return pltpu.roll(x, shift % x.shape[1], 1)
+
+
+def face(p, q):
+    both = p + q
+    return (2.0 * FINE_SCALE) * p * q / both
+
+
+def load_patch(fs, fk, fr, p, stage_u, stage_k, stage_r, sem):
+    copies = []
+    for t in range(TILES):
+        cut = pl.ds(t * 128, 128)
+        copies.append(pltpu.make_async_copy(fs.at[p, :, :, cut], stage_u.at[p, :, t], sem.at[p]))
+        copies.append(pltpu.make_async_copy(fk.at[p, :, cut], stage_k.at[p, t], sem.at[p]))
+        copies.append(pltpu.make_async_copy(fr.at[p, :, cut], stage_r.at[p, t], sem.at[p]))
+    return copies
+
+
+def patch_setup(p, stage_u, stage_k, stage_r, U, HZ, HX, HY, HM, HT, KY, KX, RT):
+    lane = lanes()
+    col = lane % 32
+    sub = lax.broadcasted_iota(jnp.int32, (8, 128), 0)
+    zero = jnp.zeros((8, 128), jnp.float32)
+    for t in range(TILES):
+        cut = pl.ds(t * 128, 128)
+        for s in range(3):
+            for j in range(RATIO):
+                U[0, s, j + 1, :, cut] = stage_u[p, s, t, pl.ds(j, 8, stride=4), :]
+    for j in range(RATIO):
+        cond = [stage_k[p, t, pl.ds(j, 8, stride=4), :] for t in range(TILES)]
+        for t in range(TILES):
+            cut = pl.ds(t * 128, 128)
+            k = cond[t]
+            RT[j, :, cut] = stage_r[p, t, pl.ds(j, 8, stride=4), :] * FINE_DT
+            if j < RATIO - 1:
+                HZ[j + 1, :, cut] = face(k, stage_k[p, t, pl.ds(j + 1, 8, stride=4), :])
+            else:
+                above = stage_k[p, t, pl.ds(0, 8, stride=4), :]
+                up = jnp.where(sub == 7, 0.0, face(k, pltpu.roll(above, 7, 0)))
+                HZ[RATIO, :, cut] = up
+                HZ[0, :, cut] = jnp.where(sub == 0, 0.0, pltpu.roll(up, 1, 0))
+            here = rot(k, -32)
+            if t < TILES - 1:
+                ahead = jnp.where(lane < 96, here, rot(cond[t + 1], -32))
+                hx = face(k, ahead)
+            else:
+                hx = jnp.where(lane < 96, face(k, here), 0.0)
+            HX[j, 0, :, cut] = hx
+            hy = jnp.where(col == 31, 0.0, face(k, rot(k, -1)))
+            HY[j, 0, :, cut] = hy
+            HY[j, 1, :, cut] = jnp.where(col == 0, 0.0, rot(hy, 1))
+            KY[j, :, cut] = jnp.where((col == 0) | (col == 31), k * FINE_SCALE, 0.0)
+        KX[j, 0] = jnp.where(lane < 32, cond[0] * FINE_SCALE, 0.0)
+        KX[j, 1] = jnp.where(lane >= 96, cond[TILES - 1] * FINE_SCALE, 0.0)
+    for j in range(RATIO):
+        last = zero
+        for t in range(TILES):
+            cut = pl.ds(t * 128, 128)
+            moved = rot(HX[j, 0, :, cut], 32)
+            behind = jnp.where(lane >= 32, moved, last)
+            last = moved
+            HX[j, 1, :, cut] = behind
+            total = (HX[j, 0, :, cut] + behind) + (HY[j, 0, :, cut] + HY[j, 1, :, cut])
+            total = total + (HZ[j, :, cut] + HZ[j + 1, :, cut]) + KY[j, :, cut]
+            if t == 0:
+                total = total + KX[j, 0]
+            if t == TILES - 1:
+                total = total + KX[j, 1]
+            HT[j, :, cut] = total
+
+
+def ghost_setup(old, new, GH):
+    lane = lanes()
+    delta = (new - old) * (1.0 / RATIO)
+    for s in range(3):
+        for t in range(TILES):
+            pick = s * 32 + 16 + t + jnp.where(lane % 32 == 31, 8, 0)
+            GH[0, s, t] = jnp.take_along_axis(old, pick, axis=1)
+            GH[1, s, t] = jnp.take_along_axis(delta, pick, axis=1)
+        pick = s * 32 + jnp.where(lane < 64, lane // 4, (lane - 96) // 4 + 8) % 16
+        GH[0, s, TILES] = jnp.take_along_axis(old, pick, axis=1)
+        GH[1, s, TILES] = jnp.take_along_axis(delta, pick, axis=1)
+
+
+def substep(now, U, HZ, HX, HY, HT, KY, KX, RT, GH):
+    lane = lanes()
+    later = 1 - now
+    for s in range(3):
+        U[now, s, 0] = pltpu.roll(U[now, s, RATIO], 1, 0)
+        U[now, s, RATIO + 1] = pltpu.roll(U[now, s, 1], 7, 0)
+
+    def plane(j, carry):
+        for t in range(TILES):
+            cut = pl.ds(t * 128, 128)
+            hzu, hzd = HZ[j + 1, :, cut], HZ[j, :, cut]
+            hxu, hxd = HX[j, 0, :, cut], HX[j, 1, :, cut]
+            hyu, hyd = HY[j, 0, :, cut], HY[j, 1, :, cut]
+            ht, ky, rt = HT[j, :, cut], KY[j, :, cut], RT[j, :, cut]
+            us = [U[now, s, j + 1, :, cut] for s in range(3)]
+            react = rt * (us[0] * us[1] - us[2])
+            for s in range(3):
+                u = us[s]
+                up = rot(u, -32)
+                if t < TILES - 1:
+                    up = jnp.where(lane < 96, up, rot(U[now, s, j + 1, :, pl.ds(t * 128 + 128, 128)], -32))
+                down = rot(u, 32)
+                if t > 0:
+                    down = jnp.where(lane >= 32, down, rot(U[now, s, j + 1, :, pl.ds(t * 128 - 128, 128)], 32))
+                flow = (hzu * U[now, s, j + 2, :, cut] + hzd * U[now, s, j, :, cut]) + (hxu * up + hxd * down)
+                flow = flow + (hyu * rot(u, -1) + hyd * rot(u, 1)) + (ky * GH[0, s, t] - ht * u)
+                if t == 0:
+                    flow = flow + KX[j, 0] * GH[0, s, TILES]
+                if t == TILES - 1:
+                    flow = flow + KX[j, 1] * GH[0, s, TILES]
+                if s > 0:
+                    flow = DIFFUSE[s] * flow
+                U[later, s, j + 1, :, cut] = u + (flow - react if s < 2 else flow + react)
+        return carry
+
+    lax.fori_loop(0, RATIO, plane, 0)
+    GH[0] = GH[0] + GH[1]
+
+
+def patch_average(final, U):
+    rows = lax.broadcasted_iota(jnp.int32, (FXY, 128), 0)
+    cols = lax.broadcasted_iota(jnp.int32, (FXY, 128), 1)
+    weights = jnp.where(cols == (rows // 128) * 8 + (rows % 32) // 4, 1.0 / 64.0, 0.0).astype(jnp.bfloat16)
+    sums = [
+        (U[final, s, 1] + U[final, s, 2]) + (U[final, s, 3] + U[final, s, 4]) for s in range(3)
+    ]
+    value = jnp.concatenate(sums, axis=0)
+    high = value.astype(jnp.bfloat16)
+    rest = value - high.astype(jnp.float32)
+    mid = rest.astype(jnp.bfloat16)
+    low = (rest - mid.astype(jnp.float32)).astype(jnp.bfloat16)
+    out = jnp.zeros((24, 128), jnp.float32)
+    for part in (low, mid, high):
+        out = out + jnp.dot(part, weights, preferred_element_type=jnp.float32)
+    return out
+
+
+def fine_kernel(fs, fk, fr, strips, out, avg, stage_u, stage_k, stage_r, result, U, HZ, HX, HY, HT, KY, KX, RT, GH, sem_in, sem_out):
+    loads = [load_patch(fs, fk, fr, p, stage_u, stage_k, stage_r, sem_in) for p in range(SLOT_DEV)]
+    for group in loads:
+        for copy in group:
+            copy.start()
+    stores = []
+    for p in range(SLOT_DEV):
+        for copy in loads[p]:
+            copy.wait()
+        patch_setup(p, stage_u, stage_k, stage_r, U, HZ, HX, HY, None, HT, KY, KX, RT)
+        ghost_setup(strips[0, p], strips[1, p], GH)
+
+        def step(k, carry):
+            substep(k % 2, U, HZ, HX, HY, HT, KY, KX, RT, GH)
+            return carry
+
+        lax.fori_loop(0, RATIO, step, 0)
+        for t in range(TILES):
+            for s in range(3):
+                for j in range(RATIO):
+                    result[p, s, t, pl.ds(j, 8, stride=4), :] = U[0, s, j + 1, :, pl.ds(t * 128, 128)]
+        for t in range(TILES):
+            copy = pltpu.make_async_copy(result.at[p, :, t], out.at[p, :, :, pl.ds(t * 128, 128)], sem_out.at[p])
+            copy.start()
+            stores.append(copy)
+        avg[p] = patch_average(0, U)
+    for copy in stores:
+        copy.wait()
+
+
+def fine(fs, fk, fr, strips):
+    f32 = jnp.float32
+    hbm = pl.BlockSpec(memory_space=pl.ANY)
+    vmem = pl.BlockSpec(memory_space=pltpu.VMEM)
+    return pl.pallas_call(
+        fine_kernel,
+        out_shape=(
+            jax.ShapeDtypeStruct((SLOT_DEV, 3, FZ, FXY), f32),
+            jax.ShapeDtypeStruct((SLOT_DEV, 24, 128), f32),
         ),
-        jnp.where(last_row, conduct, jnp.roll(conduct, -edge_len, axis=-1)),
-    )
-    prev_x = (
-        jnp.where(
-            first_row, jnp.tile(ghosts[0], (1, 1, edge_len)), jnp.roll(fields, edge_len, axis=-1)
-        ),
-        jnp.where(first_row, conduct, jnp.roll(conduct, edge_len, axis=-1)),
-    )
-    next_y = (
-        jnp.where(
-            last_col, jnp.repeat(ghosts[3], edge_len, axis=-1), jnp.roll(fields, -1, axis=-1)
-        ),
-        jnp.where(last_col, conduct, jnp.roll(conduct, -1, axis=-1)),
-    )
-    prev_y = (
-        jnp.where(
-            first_col, jnp.repeat(ghosts[2], edge_len, axis=-1), jnp.roll(fields, 1, axis=-1)
-        ),
-        jnp.where(first_col, conduct, jnp.roll(conduct, 1, axis=-1)),
-    )
-    return combine(
-        fields,
-        conduct,
-        [upward, downward, next_x, prev_x, next_y, prev_y],
-        reaction,
-        float(RATIO * RATIO),
-        DT_COARSE / RATIO,
-    )
-
-
-def restrict(fields):
-    shaped = fields.reshape(3, NZC, RATIO, BLK, RATIO, BLK, RATIO)
-    return jnp.mean(shaped, axis=(2, 4, 6)).reshape(-1)
+        in_specs=[hbm, hbm, hbm, vmem],
+        out_specs=(hbm, vmem),
+        scratch_shapes=[
+            pltpu.VMEM((SLOT_DEV, 3, TILES, FZ, 128), f32),
+            pltpu.VMEM((SLOT_DEV, TILES, FZ, 128), f32),
+            pltpu.VMEM((SLOT_DEV, TILES, FZ, 128), f32),
+            pltpu.VMEM((SLOT_DEV, 3, TILES, FZ, 128), f32),
+            pltpu.VMEM((2, 3, RATIO + 2, 8, FXY), f32),
+            pltpu.VMEM((RATIO + 1, 8, FXY), f32),
+            pltpu.VMEM((RATIO, 2, 8, FXY), f32),
+            pltpu.VMEM((RATIO, 2, 8, FXY), f32),
+            pltpu.VMEM((RATIO, 8, FXY), f32),
+            pltpu.VMEM((RATIO, 8, FXY), f32),
+            pltpu.VMEM((RATIO, 2, 8, 128), f32),
+            pltpu.VMEM((RATIO, 8, FXY), f32),
+            pltpu.VMEM((2, 3, TILES + 1, 8, 128), f32),
+            pltpu.SemaphoreType.DMA((SLOT_DEV,)),
+            pltpu.SemaphoreType.DMA((SLOT_DEV,)),
+        ],
+        compiler_params=pltpu.CompilerParams(vmem_limit_bytes=40 * 1024 * 1024),
+    )(fs, fk, fr, strips)
 
 
 def rim_rows(outer, block_cols, block_rows):
@@ -194,23 +348,16 @@
     ).astype(jnp.float32)
     earlier = rim_rows(outer_old, block_cols, block_rows)
     updated = rim_rows(outer_new, block_cols, block_rows)
-    fields = fine_state
-    for substep in range(RATIO):
-        fraction = substep / RATIO
-        current = earlier + fraction * (updated - earlier)
-        send_rows = jnp.dot(targets, current, precision=lax.Precision.HIGHEST)
-        strips = sum_sources(
-            lax.all_to_all(
-                send_rows.reshape(af_count, slot_count, current.shape[1]),
-                "af",
-                split_axis=0,
-                concat_axis=0,
-                tiled=True,
-            )
-        )
-        strips = strips.reshape(slot_count, 4, 3, NZC, BLK)
-        fields = jax.vmap(patch_step)(fields, fine_kappa, fine_rate, strips)
-    averages = jax.vmap(restrict)(fields)
+    both = jnp.concatenate([earlier, updated], axis=1)
+    send_rows = jnp.dot(targets, both, precision=lax.Precision.HIGHEST)
+    received = lax.all_to_all(
+        send_rows.reshape(af_count, slot_count, both.shape[1]), "af", split_axis=0, concat_axis=0, tiled=True
+    )
+    strips = sum_sources(received).reshape(slot_count, 2, 4, 3, NZC, BLK)
+    strips = strips.transpose(1, 0, 4, 3, 2, 5).reshape(2, slot_count, NZC, 96)
+    strips = jnp.pad(strips, ((0, 0), (0, 0), (0, 0), (0, 32)))
+    fields, averages = fine(fine_state, fine_kappa, fine_rate, strips)
+    averages = averages[:, :, :64].reshape(slot_count, -1)
     cover_mine = lax.dynamic_slice(
         cover, (af_index * block_cols, col_index * block_rows), (block_cols, block_rows)
     ).reshape(-1)

time: 608 us -> 307 us (0.50)
  the two profiles are of different devices: /device:TPU:4 before, /device:TPU:0 now
where the time goes in v1:
time: 307 us; the launch traced here: 306 us
  Pallas kernels  130 us (42%)
  blocking collectives  84.5 us (28%)
  local copies, waits for them, and re-layouts  35.1 us (11%)
  starting transfers between devices  25.8 us (8%)
  waiting for transfers between devices  18.2 us (6%)
  other arithmetic  10.2 us (3%)
    pallas_call x1, Pallas kernels, fine(): pl.pallas_call(fine_kernel, out_shape=(jax.ShapeDtypeStruct((SLOT_DEV, 3,...  130 us
    all_gather x1, blocking collectives, per_device(): portion = lax.all_gather(averages, 'af', axis=0, tiled=True)  84.5 us
    all_to_all x1, starting transfers between devices, per_device(): lax.all_to_all(send_rows.reshape(af_count, slot_count, both.shape[1]), 'a...  13.5 us
    all_to_all x1, waiting for transfers between devices, per_device(): lax.all_to_all(send_rows.reshape(af_count, slot_count, both.shape[1]), 'a...  10.5 us
    ppermute x3, starting transfers between devices, with_halo(): lax.ppermute(tail, axis, [(i, (i + 1) % count) for i in range(ends)])  8.4 us
    ppermute x3, waiting for transfers between devices, with_halo(): lax.ppermute(head, axis, [((i + 1) % count, i) for i in range(ends)])  7.6 us
  transfers between devices with their start and end apart: 7, of which 5 were waited for; matrix products, arithmetic and copies ran while one was open for 3% of the time, Pallas kernels for 0%

profile of v1, /device:TPU:0, one launch (start us, length us, event | category | flops | bytes accessed | tf_op | source)
XLA Modules:
  0.0 306.2 jit_solution(4329950561754463189)
XLA Ops:
  0.7 1.2 fusion.26
  1.9 1.4 collective-permute-start
  3.4 1.3 collective-permute-start.1
  4.7 1.8 negate_bitcast_fusion
  8.7 1.4 collective-permute-done.1
  10.7 3.5 %collective-permute-start.2 = (f32[4,8,1,258]{3,1,2,0:T(8,128)S(1)}, f32[4,8,1,258]{3,1,2,0:T(8,128)S(1)}, u32[]{:S(2)}, u32[]{:S(2)}) collective-permute-start(f32[4,8,1,258]{3,1,2,0:T(8,128)S(1)} %get-tuple-element.17), channel_id=1, source_target_pairs={{0,1},{1,2},{2,3},{3,4},{4,5},{5,6},{6,7},{7,8},{8,9},{9,10},{10,1... | collective-permute-start | bytes 99080 | tf_op jit(solution)/shard_map/ppermute | solution.py:32
  14.2 1.3 collective-permute-start.3
  16.2 4.0 %collective-permute-done.3 = f32[4,8,1,258]{3,1,2,0:T(8,128)S(1)} collective-permute-done((f32[4,8,1,258]{3,1,2,0:T(8,128)S(1)}, f32[4,8,1,258]{3,1,2,0:T(8,128)S(1)}, u32[]{:S(2)}, u32[]{:S(2)}) %collective-permute-start.3) | collective-permute-done | bytes 33056 | tf_op jit(solution)/shard_map/ppermute | solution.py:34
  21.1 1.9 slice.180
  23.0 1.9 slice.181
  24.9 1.9 slice.184
  26.8 1.9 slice.185
  29.5 1.3 fusion.15
  32.0 3.5 %collective-permute-start.4 = (f32[3,8,1,256]{3,1,2,0:T(8,128)S(1)}, f32[3,8,1,256]{3,1,2,0:T(8,128)S(1)}, u32[]{:S(2)}, u32[]{:S(2)}) collective-permute-start(f32[3,8,1,256]{3,1,2,0:T(8,128)S(1)} %copy.80), channel_id=1, source_target_pairs={{0,1},{1,2},{2,3},{3,4},{4,5},{5,6},{6,7},{7,8},{8,9},{9,10},{10,1... | collective-permute-start | bytes 73736 | tf_op jit(solution)/shard_map/ppermute | solution.py:32
  35.5 1.3 collective-permute-start.5
  39.1 2.2 collective-permute-done.5
  41.5 1.1 slice.210
  42.6 1.1 slice.211
  43.7 1.1 slice.213
  44.7 1.1 slice.214
  47.5 1.1 reshape.60
  48.6 13.5 %all-to-all-start = ((f32[32,4,1536]{2,1,0:T(4,128)}), f32[32,4,1536]{2,1,0:T(4,128)}, u32[]{:S(2)}, u32[]{:S(2)}) async-start(f32[32,4,1536]{2,1,0:T(4,128)} %reshape.60), calls=%async_computation | async-start | bytes 1572864 | tf_op jit(solution)/shard_map/all_to_all | solution.py:353
  62.1 0.9 broadcast_subtract_fusion
  64.1 10.5 %all-to-all-done = f32[32,4,1536]{2,1,0:T(4,128)} async-done(((f32[32,4,1536]{2,1,0:T(4,128)}), f32[32,4,1536]{2,1,0:T(4,128)}, u32[]{:S(2)}, u32[]{:S(2)}) %all-to-all-start) | async-done | bytes 786464 | tf_op jit(solution)/shard_map/all_to_all | solution.py:353
  74.6 1.9 reduce_sum.9
  76.5 1.0 reshape.61
  78.3 1.2 reshape.62
  79.5 129.5 %shard_map.95 = (f32[4,3,32,1024]{3,2,1,0:T(8,128)}, f32[4,24,128]{2,1,0:T(8,128)S(1)}) custom-call(f32[4,3,32,1024]{3,2,1,0:T(8,128)S(1)} %copy-done.1, f32[4,32,1024]{2,1,0:T(8,128)S(1)} %copy-done.2, f32[4,32,1024]{2,1,0:T(8,128)S(1)} %copy-done.3, f32[2,4,8,128]{3,2,1,0:T(8,128)S(1)} %pad.23.strips), custom_call_target="tpu_custom_call" | custom-call | tf_op jit(solution)/shard_map/pallas_call | solution.py:267
  209.1 84.5 %all-gather = f32[32,4,1536]{2,1,0:T(4,128)S(1)} all-gather(f32[1,4,1536]{2,1,0:T(4,128)S(1)} %reshape.66), channel_id=1, replica_groups=mesh['col'=4,'af'=32] {'af'}, dimensions={0}, use_global_device_ids=true | all-gather | bytes 811008 | tf_op jit(solution)/shard_map/all_gather | solution.py:365
  294.7 0.9 reshape.64
  295.6 3.9 %copy.93 = f32[3,8,2,8,32,8]{5,4,3,2,1,0:T(8,128)} copy(f32[3,8,2,8,32,8]{4,2,5,3,1,0:T(2,128)S(1)} %bitcast.92) | data formatting | bytes 786432 | tf_op jit(solution)/shard_map/transpose | solution.py:372
  299.5 5.7 %reshape.65 = f32[3,8,16,256]{3,2,1,0:T(8,128)S(1)} reshape(f32[3,8,2,8,32,8]{5,4,3,2,1,0:T(8,128)} %copy.93) | data formatting | bytes 786432 | tf_op jit(solution)/shard_map/reshape | solution.py:373
  (119 shorter events, 14.2 us)
Async XLA Ops:
  0.6 5.9 %copy-start = (s32[512,2]{0,1:T(2,128)S(1)}, s32[512,2]{0,1:T(2,128)}, u32[]{:S(2)}) copy-start(s32[512,2]{0,1:T(2,128)} %param.14) | copy-start | bytes 12292
  0.6 5.9 %copy-start.4 = (f32[3,8,16,256]{3,2,1,0:T(8,128)S(1)}, f32[3,8,16,256]{3,2,1,0:T(8,128)}, u32[]{:S(2)}) copy-start(f32[3,8,16,256]{3,2,1,0:T(8,128)} %param.8) | copy-start | bytes 1179652
  1.9 8.2 %copy-start.5 = (f32[8,16,256]{2,1,0:T(8,128)S(1)}, f32[8,16,256]{2,1,0:T(8,128)}, u32[]{:S(2)}) copy-start(f32[8,16,256]{2,1,0:T(8,128)} %param.9) | copy-start | bytes 393220
  1.9 6.8 %collective-permute-start = (f32[4,8,16,1]{3,2,1,0:T(8,128)S(1)}, f32[4,8,16,1]{3,2,1,0:T(8,128)S(1)}, u32[]{:S(2)}, u32[]{:S(2)}) collective-permute-start(f32[4,8,16,1]{3,2,1,0:T(8,128)S(1)} %get-tuple-element.20), channel_id=1, source_target_pairs={{0,32},{32,64},{64,96},{1,33},{33,65},{65,97},{2,34},{34,66},{66,9... | collective-permute-start | bytes 6152 | tf_op jit(solution)/shard_map/ppermute | solution.py:32
  3.4 6.8 %collective-permute-start.1 = (f32[4,8,16,1]{3,2,1,0:T(8,128)S(1)}, f32[4,8,16,1]{3,2,1,0:T(8,128)S(1)}, u32[]{:S(2)}, u32[]{:S(2)}) collective-permute-start(f32[4,8,16,1]{3,2,1,0:T(8,128)S(1)} %get-tuple-element.21), channel_id=1, source_target_pairs={{32,0},{64,32},{96,64},{33,1},{65,33},{97,65},{34,2},{66,34},{98,6... | collective-permute-start | bytes 6152 | tf_op jit(solution)/shard_map/ppermute | solution.py:34
  10.7 5.2 %collective-permute-start.2 = (f32[4,8,1,258]{3,1,2,0:T(8,128)S(1)}, f32[4,8,1,258]{3,1,2,0:T(8,128)S(1)}, u32[]{:S(2)}, u32[]{:S(2)}) collective-permute-start(f32[4,8,1,258]{3,1,2,0:T(8,128)S(1)} %get-tuple-element.17), channel_id=1, source_target_pairs={{0,1},{1,2},{2,3},{3,4},{4,5},{5,6},{6,7},{7,8},{8,9},{9,10},{10,1... | collective-permute-start | bytes 99080 | tf_op jit(solution)/shard_map/ppermute | solution.py:32
  14.2 6.0 %collective-permute-start.3 = (f32[4,8,1,258]{3,1,2,0:T(8,128)S(1)}, f32[4,8,1,258]{3,1,2,0:T(8,128)S(1)}, u32[]{:S(2)}, u32[]{:S(2)}) collective-permute-start(f32[4,8,1,258]{3,1,2,0:T(8,128)S(1)} %get-tuple-element.16), channel_id=1, source_target_pairs={{1,0},{2,1},{3,2},{4,3},{5,4},{6,5},{7,6},{8,7},{9,8},{10,9},{11,1... | collective-permute-start | bytes 99080 | tf_op jit(solution)/shard_map/ppermute | solution.py:34
  15.9 4.3 %copy-start.22 = (f32[4,8,1,258]{3,1,2,0:T(8,128)}, f32[4,8,1,258]{3,1,2,0:T(8,128)S(1)}, u32[]{:S(2)}) copy-start(f32[4,8,1,258]{3,1,2,0:T(8,128)S(1)} %collective-permute-done.2) | copy-start | bytes 99076
  20.2 0.6 copy-start.20
  28.7 0.8 copy-start.21
  28.7 0.8 copy-start.23
  30.8 0.9 copy-start.10
  30.8 1.0 copy-start.12
  30.8 6.0 %copy-start.17 = (f32[3,8,8,32]{3,1,2,0:T(8,128)S(1)}, f32[3,8,8,32]{3,1,2,0:T(8,128)}, u32[]{:S(2)}) copy-start(f32[3,8,8,32]{3,1,2,0:T(8,128)} %slice.180) | copy-start | bytes 73732
  30.8 6.1 %copy-start.16 = (f32[3,8,8,32]{3,1,2,0:T(8,128)S(1)}, f32[3,8,8,32]{3,1,2,0:T(8,128)}, u32[]{:S(2)}) copy-start(f32[3,8,8,32]{3,1,2,0:T(8,128)} %slice.181) | copy-start | bytes 73732
  31.0 6.4 %copy-start.6 = (f32[1,8,16,256]{3,2,1,0:T(8,128)}, f32[1,8,16,256]{3,2,1,0:T(8,128)S(1)}, u32[]{:S(2)}) copy-start(f32[1,8,16,256]{3,2,1,0:T(8,128)S(1)} %copy.78) | copy-start | bytes 393220
  31.0 6.4 %copy-start.8 = (f32[1,8,16,256]{3,2,1,0:T(8,128)}, f32[1,8,16,256]{3,2,1,0:T(8,128)S(1)}, u32[]{:S(2)}) copy-start(f32[1,8,16,256]{3,2,1,0:T(8,128)S(1)} %copy.79) | copy-start | bytes 393220
  31.1 6.3 %copy-start.15 = (f32[3,8,8,32]{3,1,2,0:T(8,128)S(1)}, f32[3,8,8,32]{3,1,2,0:T(8,128)}, u32[]{:S(2)}) copy-start(f32[3,8,8,32]{3,1,2,0:T(8,128)} %slice.184) | copy-start | bytes 73732
  31.8 5.7 %copy-start.14 = (f32[3,8,8,32]{3,1,2,0:T(8,128)S(1)}, f32[3,8,8,32]{3,1,2,0:T(8,128)}, u32[]{:S(2)}) copy-start(f32[3,8,8,32]{3,1,2,0:T(8,128)} %slice.185) | copy-start | bytes 73732
  31.9 6.1 %copy-start.18 = (f32[32,1,3,8,8]{0,4,3,2,1:T(8,128)S(1)}, f32[32,1,3,8,8]{0,4,3,2,1:T(8,128)}, u32[]{:S(2)}) copy-start(f32[32,1,3,8,8]{0,4,3,2,1:T(8,128)} %copy.60) | copy-start | bytes 73732
  32.0 7.0 %collective-permute-start.4 = (f32[3,8,1,256]{3,1,2,0:T(8,128)S(1)}, f32[3,8,1,256]{3,1,2,0:T(8,128)S(1)}, u32[]{:S(2)}, u32[]{:S(2)}) collective-permute-start(f32[3,8,1,256]{3,1,2,0:T(8,128)S(1)} %copy.80), channel_id=1, source_target_pairs={{0,1},{1,2},{2,3},{3,4},{4,5},{5,6},{6,7},{7,8},{8,9},{9,10},{10,1... | collective-permute-start | bytes 73736 | tf_op jit(solution)/shard_map/ppermute | solution.py:32
  35.5 5.7 %collective-permute-start.5 = (f32[3,8,1,256]{3,1,2,0:T(8,128)S(1)}, f32[3,8,1,256]{3,1,2,0:T(8,128)S(1)}, u32[]{:S(2)}, u32[]{:S(2)}) collective-permute-start(f32[3,8,1,256]{3,1,2,0:T(8,128)S(1)} %copy.81), channel_id=1, source_target_pairs={{1,0},{2,1},{3,2},{4,3},{5,4},{6,5},{7,6},{8,7},{9,8},{10,9},{11,1... | collective-permute-start | bytes 73736 | tf_op jit(solution)/shard_map/ppermute | solution.py:34
  36.9 1.1 copy-start.19
  48.6 30.9 %copy-start.3 = (f32[4,32,1024]{2,1,0:T(8,128)S(1)}, f32[4,32,1024]{2,1,0:T(8,128)}, u32[]{:S(2)}) copy-start(f32[4,32,1024]{2,1,0:T(8,128)} %fr.1) | copy-start | bytes 1572868
  48.6 26.0 %all-to-all-start = ((f32[32,4,1536]{2,1,0:T(4,128)}), f32[32,4,1536]{2,1,0:T(4,128)}, u32[]{:S(2)}, u32[]{:S(2)}) async-start(f32[32,4,1536]{2,1,0:T(4,128)} %reshape.60), calls=%async_computation | async-start | bytes 1572864 | tf_op jit(solution)/shard_map/all_to_all | solution.py:353
  62.1 17.4 %copy-start.1 = (f32[4,3,32,1024]{3,2,1,0:T(8,128)S(1)}, f32[4,3,32,1024]{3,2,1,0:T(8,128)}, u32[]{:S(2)}) copy-start(f32[4,3,32,1024]{3,2,1,0:T(8,128)} %fs.1) | copy-start | bytes 4718596
  62.1 17.4 %copy-start.2 = (f32[4,32,1024]{2,1,0:T(8,128)S(1)}, f32[4,32,1024]{2,1,0:T(8,128)}, u32[]{:S(2)}) copy-start(f32[4,32,1024]{2,1,0:T(8,128)} %fk.1) | copy-start | bytes 1572868
  299.5 5.7 %copy-start.7 = (f32[1,8,16,256]{3,2,1,0:T(8,128)S(1)}, f32[1,8,16,256]{3,2,1,0:T(8,128)}, u32[]{:S(2)}) copy-start(f32[1,8,16,256]{3,2,1,0:T(8,128)} %copy-done.6) | copy-start | bytes 393220
  299.5 5.7 %copy-start.9 = (f32[1,8,16,256]{3,2,1,0:T(8,128)S(1)}, f32[1,8,16,256]{3,2,1,0:T(8,128)}, u32[]{:S(2)}) copy-start(f32[1,8,16,256]{3,2,1,0:T(8,128)} %copy-done.8) | copy-start | bytes 393220
  299.5 5.7 %copy-start.11 = (f32[1,8,16,256]{3,2,1,0:T(8,128)S(1)}, f32[1,8,16,256]{3,2,1,0:T(8,128)}, u32[]{:S(2)}) copy-start(f32[1,8,16,256]{3,2,1,0:T(8,128)} %get-tuple-element.14) | copy-start | bytes 393220
  299.5 5.7 %copy-start.13 = (f32[8,16,256]{2,1,0:T(8,128)S(1)}, f32[8,16,256]{2,1,0:T(8,128)}, u32[]{:S(2)}) copy-start(f32[8,16,256]{2,1,0:T(8,128)} %get-tuple-element.15) | copy-start | bytes 393220

commit v2 on v1

v2 whole, which is shorter than its diff:
```python
import jax
import jax.numpy as jnp
from jax import lax
from jax.experimental import pallas as pl
from jax.experimental.pallas import tpu as pltpu
from jax.sharding import PartitionSpec as P

NZC = 8
RATIO = 4
BLK = 8
SLOT_DEV = 4
N_AF = 32
N_COL = 4
FZ = 32
FXY = 1024
TILES = FXY // 128
FINE_DT = 1.0 / 112.0
FINE_SCALE = 16.0 / 112.0


DT_COARSE = 1.0 / 28.0
DIFFUSE = (1.0, 0.7, 0.45)


def lanes(shape=(8, 128)):
    return lax.broadcasted_iota(jnp.int32, shape, 1)


def rot(x, shift):
    return pltpu.roll(x, shift % x.shape[1], 1)


def face(p, q):
    both = p + q
    return (2.0 * FINE_SCALE) * p * q / both


def load_patch(fs, fk, fr, p, stage_u, stage_k, stage_r, sem):
    copies = []
    for t in range(TILES):
        cut = pl.ds(t * 128, 128)
        copies.append(pltpu.make_async_copy(fs.at[p, :, :, cut], stage_u.at[p, :, t], sem.at[p]))
        copies.append(pltpu.make_async_copy(fk.at[p, :, cut], stage_k.at[p, t], sem.at[p]))
        copies.append(pltpu.make_async_copy(fr.at[p, :, cut], stage_r.at[p, t], sem.at[p]))
    return copies


def patch_setup(p, stage_u, stage_k, stage_r, A, HZ, HX, HY, HT, KY, KX, RT):
    lane = lanes()
    col = lane % 32
    sub = lax.broadcasted_iota(jnp.int32, (8, 128), 0)
    zero = jnp.zeros((8, 128), jnp.float32)
    for t in range(TILES):
        cut = pl.ds(t * 128, 128)
        for s in range(3):
            for j in range(RATIO):
                A[s, j + 1, :, cut] = stage_u[p, s, t, pl.ds(j, 8, stride=4), :]
    for j in range(RATIO):
        cond = [stage_k[p, t, pl.ds(j, 8, stride=4), :] for t in range(TILES)]
        for t in range(TILES):
            cut = pl.ds(t * 128, 128)
            k = cond[t]
            RT[j, :, cut] = stage_r[p, t, pl.ds(j, 8, stride=4), :] * FINE_DT
            if j < RATIO - 1:
                HZ[j + 1, :, cut] = face(k, stage_k[p, t, pl.ds(j + 1, 8, stride=4), :])
            else:
                above = stage_k[p, t, pl.ds(0, 8, stride=4), :]
                up = jnp.where(sub == 7, 0.0, face(k, pltpu.roll(above, 7, 0)))
                HZ[RATIO, :, cut] = up
                HZ[0, :, cut] = jnp.where(sub == 0, 0.0, pltpu.roll(up, 1, 0))
            here = rot(k, -32)
            if t < TILES - 1:
                ahead = jnp.where(lane < 96, here, rot(cond[t + 1], -32))
                hx = face(k, ahead)
            else:
                hx = jnp.where(lane < 96, face(k, here), 0.0)
            HX[j, 0, :, cut] = hx
            hy = jnp.where(col == 31, 0.0, face(k, rot(k, -1)))
            HY[j, 0, :, cut] = hy
            HY[j, 1, :, cut] = jnp.where(col == 0, 0.0, rot(hy, 1))
            KY[j, :, cut] = jnp.where((col == 0) | (col == 31), k * FINE_SCALE, 0.0)
        KX[j, 0] = jnp.where(lane < 32, cond[0] * FINE_SCALE, 0.0)
        KX[j, 1] = jnp.where(lane >= 96, cond[TILES - 1] * FINE_SCALE, 0.0)
    for j in range(RATIO):
        last = zero
        for t in range(TILES):
            cut = pl.ds(t * 128, 128)
            moved = rot(HX[j, 0, :, cut], 32)
            behind = jnp.where(lane >= 32, moved, last)
            last = moved
            HX[j, 1, :, cut] = behind
            total = (HX[j, 0, :, cut] + behind) + (HY[j, 0, :, cut] + HY[j, 1, :, cut])
            total = total + (HZ[j, :, cut] + HZ[j + 1, :, cut]) + KY[j, :, cut]
            if t == 0:
                total = total + KX[j, 0]
            if t == TILES - 1:
                total = total + KX[j, 1]
            HT[j, :, cut] = total


def ghost_setup(old, new, GH):
    lane = lanes()
    delta = (new - old) * (1.0 / RATIO)
    for s in range(3):
        for t in range(TILES):
            pick = s * 32 + 16 + t + jnp.where(lane % 32 == 31, 8, 0)
            GH[0, s, t] = jnp.take_along_axis(old, pick, axis=1)
            GH[1, s, t] = jnp.take_along_axis(delta, pick, axis=1)
        pick = s * 32 + jnp.where(lane < 64, lane // 4, (lane - 96) // 4 + 8) % 16
        GH[0, s, TILES] = jnp.take_along_axis(old, pick, axis=1)
        GH[1, s, TILES] = jnp.take_along_axis(delta, pick, axis=1)


def substep(A, B, HZ, HX, HY, HT, KY, KX, RT, GH):
    lane = lanes()
    for s in range(3):
        A[s, 0] = pltpu.roll(A[s, RATIO], 1, 0)
        A[s, RATIO + 1] = pltpu.roll(A[s, 1], 7, 0)

    def plane(j, carry):
        for t in range(TILES):
            cut = pl.ds(t * 128, 128)
            hzu, hzd = HZ[j + 1, :, cut], HZ[j, :, cut]
            hxu, hxd = HX[j, 0, :, cut], HX[j, 1, :, cut]
            hyu, hyd = HY[j, 0, :, cut], HY[j, 1, :, cut]
            ht, ky, rt = HT[j, :, cut], KY[j, :, cut], RT[j, :, cut]
            us = [A[s, j + 1, :, cut] for s in range(3)]
            react = rt * (us[0] * us[1] - us[2])
            for s in range(3):
                u = us[s]
                up = rot(u, -32)
                if t < TILES - 1:
                    up = jnp.where(lane < 96, up, rot(A[s, j + 1, :, pl.ds(t * 128 + 128, 128)], -32))
                down = rot(u, 32)
                if t > 0:
                    down = jnp.where(lane >= 32, down, rot(A[s, j + 1, :, pl.ds(t * 128 - 128, 128)], 32))
                flow = (hzu * A[s, j + 2, :, cut] + hzd * A[s, j, :, cut]) + (hxu * up + hxd * down)
                flow = flow + (hyu * rot(u, -1) + hyd * rot(u, 1)) + (ky * GH[0, s, t] - ht * u)
                if t == 0:
                    flow = flow + KX[j, 0] * GH[0, s, TILES]
                if t == TILES - 1:
                    flow = flow + KX[j, 1] * GH[0, s, TILES]
                if s > 0:
                    flow = DIFFUSE[s] * flow
                B[s, j + 1, :, cut] = u + (flow - react if s < 2 else flow + react)
        return carry

    lax.fori_loop(0, RATIO, plane, 0)
    GH[0] = GH[0] + GH[1]


def patch_average(A):
    rows = lax.broadcasted_iota(jnp.int32, (FXY, 128), 0)
    cols = lax.broadcasted_iota(jnp.int32, (FXY, 128), 1)
    weights = jnp.where(cols == (rows // 128) * 8 + (rows % 32) // 4, 1.0 / 64.0, 0.0).astype(jnp.bfloat16)
    sums = [
        (A[s, 1] + A[s, 2]) + (A[s, 3] + A[s, 4]) for s in range(3)
    ]
    value = jnp.concatenate(sums, axis=0)
    high = value.astype(jnp.bfloat16)
    rest = value - high.astype(jnp.float32)
    mid = rest.astype(jnp.bfloat16)
    low = (rest - mid.astype(jnp.float32)).astype(jnp.bfloat16)
    out = jnp.zeros((24, 128), jnp.float32)
    for part in (low, mid, high):
        out = out + jnp.dot(part, weights, preferred_element_type=jnp.float32)
    return out


def fine_kernel(fs, fk, fr, strips, out, avg, stage_u, stage_k, stage_r, result, A, B, HZ, HX, HY, HT, KY, KX, RT, GH, sem_in, sem_out):
    loads = [load_patch(fs, fk, fr, p, stage_u, stage_k, stage_r, sem_in) for p in range(SLOT_DEV)]
    for group in loads:
        for copy in group:
            copy.start()
    stores = []
    for p in range(SLOT_DEV):
        for copy in loads[p]:
            copy.wait()
        patch_setup(p, stage_u, stage_k, stage_r, A, HZ, HX, HY, HT, KY, KX, RT)
        ghost_setup(strips[0, p], strips[1, p], GH)

        def step(k, carry):
            substep(A, B, HZ, HX, HY, HT, KY, KX, RT, GH)
            substep(B, A, HZ, HX, HY, HT, KY, KX, RT, GH)
            return carry

        lax.fori_loop(0, RATIO // 2, step, 0)
        for t in range(TILES):
            for s in range(3):
                for j in range(RATIO):
                    result[p, s, t, pl.ds(j, 8, stride=4), :] = A[s, j + 1, :, pl.ds(t * 128, 128)]
        for t in range(TILES):
            copy = pltpu.make_async_copy(result.at[p, :, t], out.at[p, :, :, pl.ds(t * 128, 128)], sem_out.at[p])
            copy.start()
            stores.append(copy)
        value = patch_average(A)
        if p % 2 == 0:
            even = value
        else:
            for s in range(3):
                cut = slice(s * 8, s * 8 + 8)
                avg[p // 2, s] = jnp.where(lanes() < 64, even[cut], rot(value[cut], 64))
    for copy in stores:
        copy.wait()


def fine(fs, fk, fr, strips):
    f32 = jnp.float32
    hbm = pl.BlockSpec(memory_space=pl.ANY)
    vmem = pl.BlockSpec(memory_space=pltpu.VMEM)
    return pl.pallas_call(
        fine_kernel,
        out_shape=(
            jax.ShapeDtypeStruct((SLOT_DEV, 3, FZ, FXY), f32),
            jax.ShapeDtypeStruct((SLOT_DEV // 2, 3, 8, 128), f32),
        ),
        in_specs=[hbm, hbm, hbm, vmem],
        out_specs=(hbm, vmem),
        scratch_shapes=[
            pltpu.VMEM((SLOT_DEV, 3, TILES, FZ, 128), f32),
            pltpu.VMEM((SLOT_DEV, TILES, FZ, 128), f32),
            pltpu.VMEM((SLOT_DEV, TILES, FZ, 128), f32),
            pltpu.VMEM((SLOT_DEV, 3, TILES, FZ, 128), f32),
            pltpu.VMEM((3, RATIO + 2, 8, FXY), f32),
            pltpu.VMEM((3, RATIO + 2, 8, FXY), f32),
            pltpu.VMEM((RATIO + 1, 8, FXY), f32),
            pltpu.VMEM((RATIO, 2, 8, FXY), f32),
            pltpu.VMEM((RATIO, 2, 8, FXY), f32),
            pltpu.VMEM((RATIO, 8, FXY), f32),
            pltpu.VMEM((RATIO, 8, FXY), f32),
            pltpu.VMEM((RATIO, 2, 8, 128), f32),
            pltpu.VMEM((RATIO, 8, FXY), f32),
            pltpu.VMEM((2, 3, TILES + 1, 8, 128), f32),
            pltpu.SemaphoreType.DMA((SLOT_DEV,)),
            pltpu.SemaphoreType.DMA((SLOT_DEV,)),
        ],
        compiler_params=pltpu.CompilerParams(vmem_limit_bytes=40 * 1024 * 1024),
    )(fs, fk, fr, strips)


MESH = pl.DeviceIdType.MESH


def signal_partners(barrier, with_col):
    af = lax.axis_index("af")

    def tell(o, carry):
        pl.semaphore_signal(barrier, inc=1, device_id={"af": lax.rem(af + o, N_AF)}, device_id_type=MESH)
        return carry

    lax.fori_loop(1, N_AF, tell, 0)
    if with_col:
        col = lax.axis_index("col")
        for step in (1, N_COL - 1):
            pl.semaphore_signal(
                barrier, inc=1, device_id={"col": lax.rem(col + step, N_COL)}, device_id_type=MESH
            )


def safe_face(p, q):
    both = p + q
    return (2.0 * DT_COARSE) * p * q / jnp.where(both > 0.0, both, 1.0)


def swap_groups(rows, steps):
    group = lanes() // 8
    rows = list(rows)
    for d in steps:
        keep = (group & d) == 0
        for i in range(len(rows)):
            if i & d == 0:
                a, b = rows[i], rows[i + d]
                rows[i] = jnp.where(keep, a, rot(b, 8 * d))
                rows[i + d] = jnp.where(keep, rot(a, -8 * d), b)
    return rows


def pack_strips(P, base, B):
    lane = lanes((8, 256))
    within = lane % 8
    for bx in range(2):
        for half in range(2):
            cut = pl.ds(half * 128, 128)
            rows = []
            for s in range(3):
                rows.append(P[s, base + BLK * bx - 1, :, cut])
                rows.append(P[s, base + BLK * bx + BLK, :, cut])
                for turn in (1, -BLK):
                    side = jnp.zeros((8, 128), jnp.float32)
                    for a in range(BLK):
                        moved = rot(P[s, base + BLK * bx + a], a + turn)[:, half * 128 : half * 128 + 128]
                        side = jnp.where(within[:, :128] == a, moved, side)
                    rows.append(side)
            rows += rows[:4]
            for g, row in enumerate(swap_groups(rows, (8, 4, 2, 1))):
                B[bx * 32 + half * 16 + g] = row


def pack_edges(C, E):
    lane = lanes()
    low = jnp.zeros((8, 128), jnp.float32)
    high = jnp.zeros((8, 128), jnp.float32)
    for q in range(4):
        for x in range(16):
            i = q * 16 + x
            low = jnp.where(lane == i, rot(C[q, x + 2, :, 0:128], i), low)
            high = jnp.where(lane == i, rot(C[q, x + 2, :, 128:256], i + 1), high)
    E[0] = low
    E[1] = high


def edge_change(own, beyond, inside):
    lane = lanes()
    coef = safe_face(own, beyond) * inside
    spread = jnp.where(
        lane < 16,
        rot(coef, -48),
        jnp.where(lane < 32, DIFFUSE[1] * rot(coef, -32), DIFFUSE[2] * rot(coef, -16)),
    )
    return spread * (beyond - own)


def coarse_update(C, N):
    lane = lanes((8, 256))
    sub = lax.broadcasted_iota(jnp.int32, (8, 256), 0)
    before = safe_face(C[3, 0], C[3, 1])
    for xi in range(1, 19):
        k = C[3, xi]
        rate = C[4, xi] * DT_COARSE
        after = safe_face(k, C[3, xi + 1])
        hzu = jnp.where(sub == 7, 0.0, safe_face(k, pltpu.roll(k, 7, 0)))
        hzd = jnp.where(sub == 0, 0.0, pltpu.roll(hzu, 1, 0))
        hyu = jnp.where(lane == 255, 0.0, safe_face(k, rot(k, -1)))
        hyd = jnp.where(lane == 0, 0.0, rot(hyu, 1))
        total = (hzu + hzd) + (before + after) + (hyu + hyd)
        us = [C[s, xi] for s in range(3)]
        react = rate * (us[0] * us[1] - us[2])
        for s in range(3):
            u = us[s]
            flow = (hzu * pltpu.roll(u, 7, 0) + hzd * pltpu.roll(u, 1, 0)) + (
                after * C[s, xi + 1] + before * C[s, xi - 1]
            )
            flow = flow + (hyu * rot(u, -1) + hyd * rot(u, 1)) - total * u
            if s > 0:
                flow = DIFFUSE[s] * flow
            N[s, xi - 1] = u + (flow - react if s < 2 else flow + react)
        before = after


def block_row(boxes, af, col, p):
    at = col * (N_AF * SLOT_DEV) + p
    x = boxes[0, at] - af * 2
    y = boxes[1, at] - col * 32
    return jnp.where((x >= 0) & (x < 2), jnp.clip(x * 32 + y, 0, 63), 64)


def send_strips(boxes, B, SEND, RECV, send_sem, recv_sem):
    af = lax.axis_index("af")
    col = lax.axis_index("col")
    for j in range(SLOT_DEV):
        RECV[0, j] = B[block_row(boxes, af, col, af * SLOT_DEV + j)]

    def one(o, carry):
        d = lax.rem(af + o, N_AF)
        for j in range(SLOT_DEV):
            SEND[o, j] = B[block_row(boxes, af, col, d * SLOT_DEV + j)]
        spread_copy(o, d, SEND, RECV, send_sem, recv_sem).start()
        return carry

    lax.fori_loop(1, N_AF, one, 0)


def spread_copy(o, d, SEND, RECV, send_sem, recv_sem):
    return pltpu.make_async_remote_copy(
        src_ref=SEND.at[o],
        dst_ref=RECV.at[o],
        send_sem=send_sem.at[o],
        recv_sem=recv_sem.at[o],
        device_id={"af": d},
        device_id_type=MESH,
    )


def wait_all(SEND, RECV, send_sem, recv_sem):
    af = lax.axis_index("af")

    def one(o, carry):
        copy = spread_copy(o, lax.rem(af + o, N_AF), SEND, RECV, send_sem, recv_sem)
        copy.wait_send()
        copy.wait_recv()
        return carry

    lax.fori_loop(1, N_AF, one, 0)


def coarse_kernel(cs, ck, cr, boxes, strips, cnew, C, N, E, B, SEND0, SEND1, RECV0, RECV1, halo_sem, s0, r0, s1, r1):
    af = lax.axis_index("af")
    col = lax.axis_index("col")
    barrier = pltpu.get_barrier_semaphore()
    signal_partners(barrier, True)
    for s in range(3):
        C[s, 2:18] = jnp.transpose(cs[s], (1, 0, 2))
    C[3, 2:18] = jnp.transpose(ck[...], (1, 0, 2))
    C[4, 2:18] = jnp.transpose(cr[...], (1, 0, 2))
    pl.semaphore_wait(barrier, N_AF + 1)

    def halo(src, dst, sem, where):
        return pltpu.make_async_remote_copy(
            src_ref=src, dst_ref=dst, send_sem=halo_sem.at[0, sem], recv_sem=halo_sem.at[1, sem],
            device_id=where, device_id_type=MESH,
        )

    right = halo(C.at[:, 16:18], C.at[:, 0:2], 0, {"af": lax.rem(af + 1, N_AF)})
    left = halo(C.at[:, 2:4], C.at[:, 18:20], 1, {"af": lax.rem(af + N_AF - 1, N_AF)})
    right.start()
    left.start()
    pack_edges(C, E)
    down = halo(E.at[0], E.at[3], 2, {"col": lax.rem(col + N_COL - 1, N_COL)})
    up = halo(E.at[1], E.at[2], 3, {"col": lax.rem(col + 1, N_COL)})
    down.start()
    up.start()
    B[64] = jnp.zeros((8, 128), jnp.float32)
    right.wait()
    left.wait()
    C[3, 0:2] = C[3, 0:2] * (af > 0).astype(jnp.float32)
    C[3, 18:20] = C[3, 18:20] * (af < N_AF - 1).astype(jnp.float32)
    pack_strips(C, 2, B)
    send_strips(boxes, B, SEND0, RECV0, s0, r0)
    coarse_update(C, N)
    pack_strips(N, 1, B)
    send_strips(boxes, B, SEND1, RECV1, s1, r1)
    down.wait()
    up.wait()
    lane = lanes()
    change_low = edge_change(E[0], E[2], (col > 0).astype(jnp.float32))
    change_high = edge_change(E[1], E[3], (col < N_COL - 1).astype(jnp.float32))
    for s in range(3):
        for x in range(16):
            i = s * 16 + x
            cnew[s, x, :, 0:128] = N[s, x + 1, :, 0:128] + jnp.where(lane == 0, rot(change_low, -i), 0.0)
            cnew[s, x, :, 128:256] = N[s, x + 1, :, 128:256] + jnp.where(lane == 127, rot(change_high, 127 - i), 0.0)
    wait_all(SEND0, RECV0, s0, r0)
    wait_all(SEND1, RECV1, s1, r1)
    for v, RECV in ((0, RECV0), (1, RECV1)):
        for j in range(SLOT_DEV):
            strips[v, j] = lax.fori_loop(1, N_AF, lambda o, total: total + RECV[o, j], RECV[0, j])


def coarse(cs, ck, cr, boxes):
    f32 = jnp.float32
    vmem = pl.BlockSpec(memory_space=pltpu.VMEM)
    return pl.pallas_call(
        coarse_kernel,
        out_shape=(
            jax.ShapeDtypeStruct((2, SLOT_DEV, 8, 128), f32),
            jax.ShapeDtypeStruct((3, 16, 8, 256), f32),
        ),
        in_specs=[vmem, vmem, vmem, pl.BlockSpec(memory_space=pltpu.SMEM)],
        out_specs=(vmem, vmem),
        scratch_shapes=[
            pltpu.VMEM((5, 20, 8, 256), f32),
            pltpu.VMEM((3, 18, 8, 256), f32),
            pltpu.VMEM((4, 8, 128), f32),
            pltpu.VMEM((65, 8, 128), f32),
        ]
        + [pltpu.VMEM((N_AF, SLOT_DEV, 8, 128), f32)] * 4
        + [pltpu.SemaphoreType.DMA((2, 4))]
        + [pltpu.SemaphoreType.DMA((N_AF,))] * 4,
        compiler_params=pltpu.CompilerParams(
            collective_id=0, has_side_effects=True, vmem_limit_bytes=32 * 1024 * 1024
        ),
    )(cs, ck, cr, boxes)


def place_averages(cover, RECV, cnew, T):
    af = lax.axis_index("af")
    col = lax.axis_index("col")
    lane = lanes()
    group = lane // 8
    for lx in range(2):
        for h in range(2):
            own = jnp.full((8, 128), -1, jnp.int32)
            where_at = []
            for g in range(16):
                p = cover[af * 2 + lx, col * 32 + h * 16 + g]
                own = jnp.where(group == g, p, own)
                q = jnp.maximum(p - col * (N_AF * SLOT_DEV), 0)
                source = lax.div(q, SLOT_DEV)
                slot = lax.rem(q, SLOT_DEV)
                at = lax.rem(af + N_AF - source, N_AF) * 2 + lax.div(slot, 2)
                where_at.append((at, lax.rem(slot, 2)))
            covered = own >= 0
            for s in range(3):
                rows = []
                for g in range(8):
                    at, odd = where_at[g]
                    first = RECV[at, s]
                    first = jnp.where(odd == 1, rot(first, 64), first)
                    at, odd = where_at[g + 8]
                    second = RECV[at, s]
                    second = jnp.where(odd == 1, second, rot(second, 64))
                    rows.append(jnp.where(lane < 64, first, second))
                for x, row in enumerate(swap_groups(rows, (4, 2, 1))):
                    cut = pl.ds(h * 128, 128)
                    T[s, lx * BLK + x, :, cut] = jnp.where(covered, row, cnew[s, lx * BLK + x, :, cut])


def average_kernel(avg, cnew, cover, out, T, RECV, send_sem, recv_sem):
    af = lax.axis_index("af")
    barrier = pltpu.get_barrier_semaphore()
    signal_partners(barrier, False)
    RECV[0:2] = avg[...]
    pl.semaphore_wait(barrier, N_AF - 1)

    def copy(o):
        return pltpu.make_async_remote_copy(
            src_ref=avg,
            dst_ref=RECV.at[pl.ds(o * 2, 2)],
            send_sem=send_sem.at[o],
            recv_sem=recv_sem.at[o],
            device_id={"af": lax.rem(af + o, N_AF)},
            device_id_type=MESH,
        )

    def begin(o, carry):
        copy(o).start()
        return carry

    def finish(o, carry):
        copy(o).wait_send()
        copy(o).wait_recv()
        return carry

    lax.fori_loop(1, N_AF, begin, 0)
    lax.fori_loop(1, N_AF, finish, 0)
    place_averages(cover, RECV, cnew, T)
    for s in range(3):
        out[s] = jnp.transpose(T[s], (1, 0, 2))


def averages_to_coarse(avg, cnew, cover):
    f32 = jnp.float32
    vmem = pl.BlockSpec(memory_space=pltpu.VMEM)
    return pl.pallas_call(
        average_kernel,
        out_shape=jax.ShapeDtypeStruct((3, NZC, 16, 256), f32),
        in_specs=[vmem, vmem, pl.BlockSpec(memory_space=pltpu.SMEM)],
        out_specs=vmem,
        scratch_shapes=[
            pltpu.VMEM((3, 16, 8, 256), f32),
            pltpu.VMEM((N_AF * 2, 3, 8, 128), f32),
            pltpu.SemaphoreType.DMA((N_AF,)),
            pltpu.SemaphoreType.DMA((N_AF,)),
        ],
        compiler_params=pltpu.CompilerParams(
            collective_id=1, has_side_effects=True, vmem_limit_bytes=32 * 1024 * 1024
        ),
    )(avg, cnew, cover)


def per_device(
    coarse_state, coarse_kappa, coarse_rate, fine_state, fine_kappa, fine_rate, boxes, cover
):
    strips, cnew = coarse(coarse_state, coarse_kappa, coarse_rate, boxes.T)
    fields, avg = fine(fine_state, fine_kappa, fine_rate, strips)
    return averages_to_coarse(avg, cnew, cover), fields


def solution(mesh):
    return jax.shard_map(
        per_device,
        mesh=mesh,
        in_specs=(
            P(None, None, "af", "col"),
            P(None, "af", "col"),
            P(None, "af", "col"),
            P(("col", "af"), None, None, None),
            P(("col", "af"), None, None),
            P(("col", "af"), None, None),
            P(),
            P(),
        ),
        out_specs=(P(None, None, "af", "col"), P(("col", "af"), None, None, None)),
        check_vma=False,
    )
```

time: 307 us -> 79.5 us (0.26)
  blocking collectives: 84.5 us -> 0 us
  Pallas kernels: 130 us -> 69.9 us
  local copies, waits for them, and re-layouts: 35.1 us -> 7.72 us
  starting transfers between devices: 25.8 us -> 0 us
  waiting for transfers between devices: 18.2 us -> 0 us
  other arithmetic: 10.2 us -> 0 us
    pallas_call x1, Pallas kernels: 130 us -> 20.1 us  [fine(): pl.pallas_call(fine_kernel, out_shape=(jax.ShapeDtypeStruct((SLOT_DEV, 3,...]
    all_gather x1 -> x0, blocking collectives: 84.5 us -> none  [per_device(): portion = lax.all_gather(averages, 'af', axis=0, tiled=True)]
    pallas_call x0 -> x2, Pallas kernels: none -> 49.8 us  [the longest x1 30.1 us: coarse(): pl.pallas_call(coarse_kernel, out_shape=(jax.ShapeDtypeStruct((2, SLOT_DE...]
    all_to_all x1 -> x0, starting transfers between devices: 13.5 us -> none  [per_device(): lax.all_to_all(send_rows.reshape(af_count, slot_count, both.shape[1]), 'a...]
    slice x18 -> x0, local copies, waits for them, and re-layouts: 12.6 us -> none  [the longest x4 5.97 us: rim_rows(): padded_y[:, :, base_x + 1:base_x + 1 + BLK, 0:cells_y:BLK]]
    ppermute x6 -> x0, starting transfers between devices: 12.3 us -> none  [the longest x3 8.4 us: with_halo(): lax.ppermute(tail, axis, [(i, (i + 1) % count) for i in range(ends)])]
    all_to_all x1 -> x0, waiting for transfers between devices: 10.5 us -> none  [per_device(): lax.all_to_all(send_rows.reshape(af_count, slot_count, both.shape[1]), 'a...]
    reshape x7 -> x0, local copies, waits for them, and re-layouts: 9.94 us -> none  [the longest x1 5.67 us: per_device(): placed = placed.reshape(block_cols, block_rows, 3, NZC, BLK, BLK).transpo...]
  transfers between devices with their start and end apart: 7 -> 0, of which waited for: 5 -> 0; matrix products, arithmetic and copies ran while one was open for 3% -> 0% of each run, Pallas kernels for 0% -> 0%
where the time goes in v2:
time: 79.5 us; the launch traced here: 78.3 us
  Pallas kernels  69.9 us (88%)
  local copies, waits for them, and re-layouts  7.72 us (10%)
    pallas_call x1, Pallas kernels, coarse(): pl.pallas_call(coarse_kernel, out_shape=(jax.ShapeDtypeStruct((2, SLOT_DE...  30.1 us
    pallas_call x1, Pallas kernels, fine(): pl.pallas_call(fine_kernel, out_shape=(jax.ShapeDtypeStruct((SLOT_DEV, 3,...  20.1 us
    pallas_call x1, Pallas kernels, averages_to_coarse(): pl.pallas_call(average_kernel, out_shape=jax.ShapeDtypeStruct((3, NZC, 16...  19.7 us
    unnamed x17, local copies, waits for them, and re-layouts  7.72 us

profile of v2, /device:TPU:0, one launch (start us, length us, event | category | flops | bytes accessed | tf_op | source)
XLA Modules:
  0.0 78.3 jit_solution(9922352465026448245)
XLA Ops:
  0.6 0.0 copy-start.3
  0.6 1.0 %copy-done.3 = f32[3,8,16,256]{3,2,1,0:T(8,128)S(1)} copy-done((f32[3,8,16,256]{3,2,1,0:T(8,128)S(1)}, f32[3,8,16,256]{3,2,1,0:T(8,128)}, u32[]{:S(2)}) %copy-start.3) | copy-done | bytes 393240
  1.6 0.0 copy-start.4
  1.6 0.9 %copy-done.4 = f32[8,16,256]{2,1,0:T(8,128)S(1)} copy-done((f32[8,16,256]{2,1,0:T(8,128)S(1)}, f32[8,16,256]{2,1,0:T(8,128)}, u32[]{:S(2)}) %copy-start.4) | copy-done | bytes 131096
  2.5 0.0 copy-start.5
  2.5 0.9 %copy-done.5 = f32[8,16,256]{2,1,0:T(8,128)S(1)} copy-done((f32[8,16,256]{2,1,0:T(8,128)S(1)}, f32[8,16,256]{2,1,0:T(8,128)}, u32[]{:S(2)}) %copy-start.5) | copy-done | bytes 131096
  3.4 0.0 copy-start.7
  3.4 0.7 copy-done.7
  4.1 0.0 copy-start.6
  4.1 30.1 %shard_map.95 = (f32[2,4,8,128]{3,2,1,0:T(8,128)S(1)}, f32[3,16,8,256]{3,2,1,0:T(8,128)S(1)}) custom-call(f32[3,8,16,256]{3,2,1,0:T(8,128)S(1)} %copy-done.3, f32[8,16,256]{2,1,0:T(8,128)S(1)} %copy-done.4, f32[8,16,256]{2,1,0:T(8,128)S(1)} %copy-done.5, s32[2,512]{1,0:T(2,128)S(1)} %bitcast.1), custom_call_target="tpu_custom_call" | custom-call | tf_op jit(solution)/shard_map/pallas_call | solution.py:452
  34.2 0.0 copy-start
  34.2 1.4 %copy-done = f32[4,3,32,1024]{3,2,1,0:T(8,128)S(1)} copy-done((f32[4,3,32,1024]{3,2,1,0:T(8,128)S(1)}, f32[4,3,32,1024]{3,2,1,0:T(8,128)}, u32[]{:S(2)}) %copy-start) | copy-done | bytes 1572888
  35.6 0.0 copy-start.1
  35.6 1.0 %copy-done.1 = f32[4,32,1024]{2,1,0:T(8,128)S(1)} copy-done((f32[4,32,1024]{2,1,0:T(8,128)S(1)}, f32[4,32,1024]{2,1,0:T(8,128)}, u32[]{:S(2)}) %copy-start.1) | copy-done | bytes 524312
  36.7 0.0 copy-start.2
  36.7 1.0 %copy-done.2 = f32[4,32,1024]{2,1,0:T(8,128)S(1)} copy-done((f32[4,32,1024]{2,1,0:T(8,128)S(1)}, f32[4,32,1024]{2,1,0:T(8,128)}, u32[]{:S(2)}) %copy-start.2) | copy-done | bytes 524312
  37.7 20.1 %shard_map.96 = (f32[4,3,32,1024]{3,2,1,0:T(8,128)}, f32[2,3,8,128]{3,2,1,0:T(8,128)S(1)}) custom-call(f32[4,3,32,1024]{3,2,1,0:T(8,128)S(1)} %copy-done, f32[4,32,1024]{2,1,0:T(8,128)S(1)} %copy-done.1, f32[4,32,1024]{2,1,0:T(8,128)S(1)} %copy-done.2, f32[2,4,8,128]{3,2,1,0:T(8,128)S(1)} %get-tuple-element.6.strips), custom_call_target="tpu_custom_call" | custom-call | tf_op jit(solution)/shard_map/pallas_call | solution.py:211
  57.9 0.0 copy-done.6
  57.9 19.7 %shard_map.97 = f32[3,8,16,256]{3,2,1,0:T(8,128)S(1)} custom-call(f32[2,3,8,128]{3,2,1,0:T(8,128)S(1)} %get-tuple-element.7.avg, f32[3,16,8,256]{3,2,1,0:T(8,128)S(1)} %get-tuple-element.8.cnew, s32[64,128]{1,0:T(8,128)S(1)} %copy-done.6), custom_call_target="tpu_custom_call" | custom-call | tf_op jit(solution)/shard_map/pallas_call | solution.py:544
  77.6 0.7 copy.11
Async XLA Ops:
  0.6 1.0 %copy-start.3 = (f32[3,8,16,256]{3,2,1,0:T(8,128)S(1)}, f32[3,8,16,256]{3,2,1,0:T(8,128)}, u32[]{:S(2)}) copy-start(f32[3,8,16,256]{3,2,1,0:T(8,128)} %cs.1) | copy-start | bytes 1179652
  1.6 0.9 %copy-start.4 = (f32[8,16,256]{2,1,0:T(8,128)S(1)}, f32[8,16,256]{2,1,0:T(8,128)}, u32[]{:S(2)}) copy-start(f32[8,16,256]{2,1,0:T(8,128)} %ck.1) | copy-start | bytes 393220
  2.5 0.9 %copy-start.5 = (f32[8,16,256]{2,1,0:T(8,128)S(1)}, f32[8,16,256]{2,1,0:T(8,128)}, u32[]{:S(2)}) copy-start(f32[8,16,256]{2,1,0:T(8,128)} %cr.1) | copy-start | bytes 393220
  3.4 0.7 copy-start.7
  4.1 53.7 %copy-start.6 = (s32[64,128]{1,0:T(8,128)S(1)}, s32[64,128]{1,0:T(8,128)}, u32[]{:S(2)}) copy-start(s32[64,128]{1,0:T(8,128)} %cover.1) | copy-start | bytes 98308
  34.2 1.4 %copy-start = (f32[4,3,32,1024]{3,2,1,0:T(8,128)S(1)}, f32[4,3,32,1024]{3,2,1,0:T(8,128)}, u32[]{:S(2)}) copy-start(f32[4,3,32,1024]{3,2,1,0:T(8,128)} %fs.1) | copy-start | bytes 4718596
  35.6 1.0 %copy-start.1 = (f32[4,32,1024]{2,1,0:T(8,128)S(1)}, f32[4,32,1024]{2,1,0:T(8,128)}, u32[]{:S(2)}) copy-start(f32[4,32,1024]{2,1,0:T(8,128)} %fk.1) | copy-start | bytes 1572868
  36.7 1.0 %copy-start.2 = (f32[4,32,1024]{2,1,0:T(8,128)S(1)}, f32[4,32,1024]{2,1,0:T(8,128)}, u32[]{:S(2)}) copy-start(f32[4,32,1024]{2,1,0:T(8,128)} %fr.1) | copy-start | bytes 1572868

commit v3 on v2

--- a/solution.py
+++ b/solution.py
@@ -43,6 +43,13 @@
         copies.append(pltpu.make_async_copy(fk.at[p, :, cut], stage_k.at[p, t], sem.at[p]))
         copies.append(pltpu.make_async_copy(fr.at[p, :, cut], stage_r.at[p, t], sem.at[p]))
     return copies
+
+
+def store_patch(result, out, p, sem):
+    return [
+        pltpu.make_async_copy(result.at[p, :, t], out.at[p, :, :, pl.ds(t * 128, 128)], sem.at[p])
+        for t in range(TILES)
+    ]
 
 
 def patch_setup(p, stage_u, stage_k, stage_r, A, HZ, HX, HY, HT, KY, KX, RT):
@@ -98,17 +105,14 @@
             HT[j, :, cut] = total
 
 
-def ghost_setup(old, new, GH):
+def ghost_tiles(strip, GH):
     lane = lanes()
-    delta = (new - old) * (1.0 / RATIO)
     for s in range(3):
         for t in range(TILES):
             pick = s * 32 + 16 + t + jnp.where(lane % 32 == 31, 8, 0)
-            GH[0, s, t] = jnp.take_along_axis(old, pick, axis=1)
-            GH[1, s, t] = jnp.take_along_axis(delta, pick, axis=1)
+            GH[s, t] = jnp.take_along_axis(strip, pick, axis=1)
         pick = s * 32 + jnp.where(lane < 64, lane // 4, (lane - 96) // 4 + 8) % 16
-        GH[0, s, TILES] = jnp.take_along_axis(old, pick, axis=1)
-        GH[1, s, TILES] = jnp.take_along_axis(delta, pick, axis=1)
+        GH[s, TILES] = jnp.take_along_axis(strip, pick, axis=1)
 
 
 def substep(A, B, HZ, HX, HY, HT, KY, KX, RT, GH):
@@ -118,35 +122,38 @@
         A[s, RATIO + 1] = pltpu.roll(A[s, 1], 7, 0)
 
     def plane(j, carry):
+        mid = [[A[s, j + 1, :, pl.ds(t * 128, 128)] for t in range(TILES)] for s in range(3)]
+        ups = [[rot(u, -32) for u in mid[s]] for s in range(3)]
+        downs = [[rot(u, 32) for u in mid[s]] for s in range(3)]
         for t in range(TILES):
             cut = pl.ds(t * 128, 128)
             hzu, hzd = HZ[j + 1, :, cut], HZ[j, :, cut]
             hxu, hxd = HX[j, 0, :, cut], HX[j, 1, :, cut]
             hyu, hyd = HY[j, 0, :, cut], HY[j, 1, :, cut]
             ht, ky, rt = HT[j, :, cut], KY[j, :, cut], RT[j, :, cut]
-            us = [A[s, j + 1, :, cut] for s in range(3)]
+            us = [mid[s][t] for s in range(3)]
             react = rt * (us[0] * us[1] - us[2])
             for s in range(3):
                 u = us[s]
-                up = rot(u, -32)
+                up = ups[s][t]
                 if t < TILES - 1:
-                    up = jnp.where(lane < 96, up, rot(A[s, j + 1, :, pl.ds(t * 128 + 128, 128)], -32))
-                down = rot(u, 32)
+                    up = jnp.where(lane < 96, up, ups[s][t + 1])
+                down = downs[s][t]
                 if t > 0:
-                    down = jnp.where(lane >= 32, down, rot(A[s, j + 1, :, pl.ds(t * 128 - 128, 128)], 32))
+                    down = jnp.where(lane >= 32, down, downs[s][t - 1])
                 flow = (hzu * A[s, j + 2, :, cut] + hzd * A[s, j, :, cut]) + (hxu * up + hxd * down)
-                flow = flow + (hyu * rot(u, -1) + hyd * rot(u, 1)) + (ky * GH[0, s, t] - ht * u)
+                flow = flow + (hyu * rot(u, -1) + hyd * rot(u, 1)) + (ky * GH[s, t] - ht * u)
                 if t == 0:
-                    flow = flow + KX[j, 0] * GH[0, s, TILES]
+                    flow = flow + KX[j, 0] * GH[s, TILES]
                 if t == TILES - 1:
-                    flow = flow + KX[j, 1] * GH[0, s, TILES]
+                    flow = flow + KX[j, 1] * GH[s, TILES]
                 if s > 0:
                     flow = DIFFUSE[s] * flow
                 B[s, j + 1, :, cut] = u + (flow - react if s < 2 else flow + react)
         return carry
 
-    lax.fori_loop(0, RATIO, plane, 0)
-    GH[0] = GH[0] + GH[1]
+    for j in range(RATIO):
+        plane(j, 0)
 
 
 def patch_average(A):
@@ -165,77 +172,6 @@
     for part in (low, mid, high):
         out = out + jnp.dot(part, weights, preferred_element_type=jnp.float32)
     return out
-
-
-def fine_kernel(fs, fk, fr, strips, out, avg, stage_u, stage_k, stage_r, result, A, B, HZ, HX, HY, HT, KY, KX, RT, GH, sem_in, sem_out):
-    loads = [load_patch(fs, fk, fr, p, stage_u, stage_k, stage_r, sem_in) for p in range(SLOT_DEV)]
-    for group in loads:
-        for copy in group:
-            copy.start()
-    stores = []
-    for p in range(SLOT_DEV):
-        for copy in loads[p]:
-            copy.wait()
-        patch_setup(p, stage_u, stage_k, stage_r, A, HZ, HX, HY, HT, KY, KX, RT)
-        ghost_setup(strips[0, p], strips[1, p], GH)
-
-        def step(k, carry):
-            substep(A, B, HZ, HX, HY, HT, KY, KX, RT, GH)
-            substep(B, A, HZ, HX, HY, HT, KY, KX, RT, GH)
-            return carry
-
-        lax.fori_loop(0, RATIO // 2, step, 0)
-        for t in range(TILES):
-            for s in range(3):
-                for j in range(RATIO):
-                    result[p, s, t, pl.ds(j, 8, stride=4), :] = A[s, j + 1, :, pl.ds(t * 128, 128)]
-        for t in range(TILES):
-            copy = pltpu.make_async_copy(result.at[p, :, t], out.at[p, :, :, pl.ds(t * 128, 128)], sem_out.at[p])
-            copy.start()
-            stores.append(copy)
-        value = patch_average(A)
-        if p % 2 == 0:
-            even = value
-        else:
-            for s in range(3):
-                cut = slice(s * 8, s * 8 + 8)
-                avg[p // 2, s] = jnp.where(lanes() < 64, even[cut], rot(value[cut], 64))
-    for copy in stores:
-        copy.wait()
-
-
-def fine(fs, fk, fr, strips):
-    f32 = jnp.float32
-    hbm = pl.BlockSpec(memory_space=pl.ANY)
-    vmem = pl.BlockSpec(memory_space=pltpu.VMEM)
-    return pl.pallas_call(
-        fine_kernel,
-        out_shape=(
-            jax.ShapeDtypeStruct((SLOT_DEV, 3, FZ, FXY), f32),
-            jax.ShapeDtypeStruct((SLOT_DEV // 2, 3, 8, 128), f32),
-        ),
-        in_specs=[hbm, hbm, hbm, vmem],
-        out_specs=(hbm, vmem),
-        scratch_shapes=[
-            pltpu.VMEM((SLOT_DEV, 3, TILES, FZ, 128), f32),
-            pltpu.VMEM((SLOT_DEV, TILES, FZ, 128), f32),
-            pltpu.VMEM((SLOT_DEV, TILES, FZ, 128), f32),
-            pltpu.VMEM((SLOT_DEV, 3, TILES, FZ, 128), f32),
-            pltpu.VMEM((3, RATIO + 2, 8, FXY), f32),
-            pltpu.VMEM((3, RATIO + 2, 8, FXY), f32),
-            pltpu.VMEM((RATIO + 1, 8, FXY), f32),
-            pltpu.VMEM((RATIO, 2, 8, FXY), f32),
-            pltpu.VMEM((RATIO, 2, 8, FXY), f32),
-            pltpu.VMEM((RATIO, 8, FXY), f32),
-            pltpu.VMEM((RATIO, 8, FXY), f32),
-            pltpu.VMEM((RATIO, 2, 8, 128), f32),
-            pltpu.VMEM((RATIO, 8, FXY), f32),
-            pltpu.VMEM((2, 3, TILES + 1, 8, 128), f32),
-            pltpu.SemaphoreType.DMA((SLOT_DEV,)),
-            pltpu.SemaphoreType.DMA((SLOT_DEV,)),
-        ],
-        compiler_params=pltpu.CompilerParams(vmem_limit_bytes=40 * 1024 * 1024),
-    )(fs, fk, fr, strips)
 
 
 MESH = pl.DeviceIdType.MESH
@@ -393,85 +329,6 @@
     lax.fori_loop(1, N_AF, one, 0)
 
 
-def coarse_kernel(cs, ck, cr, boxes, strips, cnew, C, N, E, B, SEND0, SEND1, RECV0, RECV1, halo_sem, s0, r0, s1, r1):
-    af = lax.axis_index("af")
-    col = lax.axis_index("col")
-    barrier = pltpu.get_barrier_semaphore()
-    signal_partners(barrier, True)
-    for s in range(3):
-        C[s, 2:18] = jnp.transpose(cs[s], (1, 0, 2))
-    C[3, 2:18] = jnp.transpose(ck[...], (1, 0, 2))
-    C[4, 2:18] = jnp.transpose(cr[...], (1, 0, 2))
-    pl.semaphore_wait(barrier, N_AF + 1)
-
-    def halo(src, dst, sem, where):
-        return pltpu.make_async_remote_copy(
-            src_ref=src, dst_ref=dst, send_sem=halo_sem.at[0, sem], recv_sem=halo_sem.at[1, sem],
-            device_id=where, device_id_type=MESH,
-        )
-
-    right = halo(C.at[:, 16:18], C.at[:, 0:2], 0, {"af": lax.rem(af + 1, N_AF)})
-    left = halo(C.at[:, 2:4], C.at[:, 18:20], 1, {"af": lax.rem(af + N_AF - 1, N_AF)})
-    right.start()
-    left.start()
-    pack_edges(C, E)
-    down = halo(E.at[0], E.at[3], 2, {"col": lax.rem(col + N_COL - 1, N_COL)})
-    up = halo(E.at[1], E.at[2], 3, {"col": lax.rem(col + 1, N_COL)})
-    down.start()
-    up.start()
-    B[64] = jnp.zeros((8, 128), jnp.float32)
-    right.wait()
-    left.wait()
-    C[3, 0:2] = C[3, 0:2] * (af > 0).astype(jnp.float32)
-    C[3, 18:20] = C[3, 18:20] * (af < N_AF - 1).astype(jnp.float32)
-    pack_strips(C, 2, B)
-    send_strips(boxes, B, SEND0, RECV0, s0, r0)
-    coarse_update(C, N)
-    pack_strips(N, 1, B)
-    send_strips(boxes, B, SEND1, RECV1, s1, r1)
-    down.wait()
-    up.wait()
-    lane = lanes()
-    change_low = edge_change(E[0], E[2], (col > 0).astype(jnp.float32))
-    change_high = edge_change(E[1], E[3], (col < N_COL - 1).astype(jnp.float32))
-    for s in range(3):
-        for x in range(16):
-            i = s * 16 + x
-            cnew[s, x, :, 0:128] = N[s, x + 1, :, 0:128] + jnp.where(lane == 0, rot(change_low, -i), 0.0)
-            cnew[s, x, :, 128:256] = N[s, x + 1, :, 128:256] + jnp.where(lane == 127, rot(change_high, 127 - i), 0.0)
-    wait_all(SEND0, RECV0, s0, r0)
-    wait_all(SEND1, RECV1, s1, r1)
-    for v, RECV in ((0, RECV0), (1, RECV1)):
-        for j in range(SLOT_DEV):
-            strips[v, j] = lax.fori_loop(1, N_AF, lambda o, total: total + RECV[o, j], RECV[0, j])
-
-
-def coarse(cs, ck, cr, boxes):
-    f32 = jnp.float32
-    vmem = pl.BlockSpec(memory_space=pltpu.VMEM)
-    return pl.pallas_call(
-        coarse_kernel,
-        out_shape=(
-            jax.ShapeDtypeStruct((2, SLOT_DEV, 8, 128), f32),
-            jax.ShapeDtypeStruct((3, 16, 8, 256), f32),
-        ),
-        in_specs=[vmem, vmem, vmem, pl.BlockSpec(memory_space=pltpu.SMEM)],
-        out_specs=(vmem, vmem),
-        scratch_shapes=[
-            pltpu.VMEM((5, 20, 8, 256), f32),
-            pltpu.VMEM((3, 18, 8, 256), f32),
-            pltpu.VMEM((4, 8, 128), f32),
-            pltpu.VMEM((65, 8, 128), f32),
-        ]
-        + [pltpu.VMEM((N_AF, SLOT_DEV, 8, 128), f32)] * 4
-        + [pltpu.SemaphoreType.DMA((2, 4))]
-        + [pltpu.SemaphoreType.DMA((N_AF,))] * 4,
-        compiler_params=pltpu.CompilerParams(
-            collective_id=0, has_side_effects=True, vmem_limit_bytes=32 * 1024 * 1024
-        ),
-    )(cs, ck, cr, boxes)
-
-
 def place_averages(cover, RECV, cnew, T):
     af = lax.axis_index("af")
     col = lax.axis_index("col")
@@ -487,83 +344,242 @@
                 q = jnp.maximum(p - col * (N_AF * SLOT_DEV), 0)
                 source = lax.div(q, SLOT_DEV)
                 slot = lax.rem(q, SLOT_DEV)
-                at = lax.rem(af + N_AF - source, N_AF) * 2 + lax.div(slot, 2)
+                at = (lax.div(slot, 2), lax.rem(af + N_AF - source, N_AF))
                 where_at.append((at, lax.rem(slot, 2)))
             covered = own >= 0
             for s in range(3):
                 rows = []
                 for g in range(8):
                     at, odd = where_at[g]
-                    first = RECV[at, s]
+                    first = RECV[at[0], at[1], s]
                     first = jnp.where(odd == 1, rot(first, 64), first)
                     at, odd = where_at[g + 8]
-                    second = RECV[at, s]
+                    second = RECV[at[0], at[1], s]
                     second = jnp.where(odd == 1, second, rot(second, 64))
                     rows.append(jnp.where(lane < 64, first, second))
                 for x, row in enumerate(swap_groups(rows, (4, 2, 1))):
                     cut = pl.ds(h * 128, 128)
-                    T[s, lx * BLK + x, :, cut] = jnp.where(covered, row, cnew[s, lx * BLK + x, :, cut])
-
-
-def average_kernel(avg, cnew, cover, out, T, RECV, send_sem, recv_sem):
+                    T[s, lx * BLK + x, :, cut] = jnp.where(covered, row, cnew[s, lx * BLK + x + 1, :, cut])
+
+
+def total_of(RECV, j):
+    return lax.fori_loop(1, N_AF, lambda o, total: total + RECV[o, j], RECV[0, j])
+
+
+def kernel(
+    cs, ck, cr, fs, fk, fr, boxes_in, cover_in, coarse_out, fine_out,
+    boxes, cover, CI, C, N, T, E, BLOCKS, SEND0, SEND1, RECV0, RECV1, PAIR, AVG, RECVA,
+    stage_u, stage_k, stage_r, result, A, B, HZ, HX, HY, HT, KY, KX, RT, GH, ST,
+    load_sem, halo_sem, s0, r0, s1, r1, sa, ra, sem_in, sem_out,
+):
     af = lax.axis_index("af")
+    col = lax.axis_index("col")
     barrier = pltpu.get_barrier_semaphore()
-    signal_partners(barrier, False)
-    RECV[0:2] = avg[...]
-    pl.semaphore_wait(barrier, N_AF - 1)
-
-    def copy(o):
+    first = [
+        pltpu.make_async_copy(cs, CI.at[0:3], load_sem.at[0]),
+        pltpu.make_async_copy(ck, CI.at[3], load_sem.at[1]),
+        pltpu.make_async_copy(cr, CI.at[4], load_sem.at[2]),
+        pltpu.make_async_copy(boxes_in, boxes, load_sem.at[3]),
+        pltpu.make_async_copy(cover_in, cover, load_sem.at[4]),
+    ]
+    for copy in first:
+        copy.start()
+    signal_partners(barrier, True)
+
+    def begin_load(p, carry):
+        for copy in load_patch(fs, fk, fr, p, stage_u, stage_k, stage_r, sem_in):
+            copy.start()
+        return carry
+
+    lax.fori_loop(0, SLOT_DEV, begin_load, 0)
+    for copy in first:
+        copy.wait()
+    for q in range(5):
+        C[q, 2:18] = jnp.transpose(CI[q], (1, 0, 2))
+    pl.semaphore_wait(barrier, N_AF + 1)
+
+    def halo(src, dst, sem, where):
         return pltpu.make_async_remote_copy(
-            src_ref=avg,
-            dst_ref=RECV.at[pl.ds(o * 2, 2)],
-            send_sem=send_sem.at[o],
-            recv_sem=recv_sem.at[o],
+            src_ref=src, dst_ref=dst, send_sem=halo_sem.at[0, sem], recv_sem=halo_sem.at[1, sem],
+            device_id=where, device_id_type=MESH,
+        )
+
+    right = halo(C.at[:, 16:18], C.at[:, 0:2], 0, {"af": lax.rem(af + 1, N_AF)})
+    left = halo(C.at[:, 2:4], C.at[:, 18:20], 1, {"af": lax.rem(af + N_AF - 1, N_AF)})
+    right.start()
+    left.start()
+    pack_edges(C, E)
+    down = halo(E.at[0], E.at[3], 2, {"col": lax.rem(col + N_COL - 1, N_COL)})
+    up = halo(E.at[1], E.at[2], 3, {"col": lax.rem(col + 1, N_COL)})
+    down.start()
+    up.start()
+    BLOCKS[64] = jnp.zeros((8, 128), jnp.float32)
+    right.wait()
+    left.wait()
+    C[3, 0:2] = C[3, 0:2] * (af > 0).astype(jnp.float32)
+    C[3, 18:20] = C[3, 18:20] * (af < N_AF - 1).astype(jnp.float32)
+    pack_strips(C, 2, BLOCKS)
+    send_strips(boxes, BLOCKS, SEND0, RECV0, s0, r0)
+    coarse_update(C, N)
+    pack_strips(N, 1, BLOCKS)
+    send_strips(boxes, BLOCKS, SEND1, RECV1, s1, r1)
+
+    def prepare(p, carry):
+        for copy in load_patch(fs, fk, fr, p, stage_u, stage_k, stage_r, sem_in):
+            copy.wait()
+        patch_setup(p, stage_u, stage_k, stage_r, A.at[p], HZ.at[p], HX.at[p], HY.at[p], HT.at[p], KY.at[p], KX.at[p], RT.at[p])
+        return carry
+
+    lax.fori_loop(0, SLOT_DEV, prepare, 0)
+    wait_all(SEND0, RECV0, s0, r0)
+
+    def opening(p, carry):
+        ST[0, p] = total_of(RECV0, p)
+        ghost_tiles(ST[0, p], GH.at[p])
+        substep(A.at[p], B.at[p], HZ.at[p], HX.at[p], HY.at[p], HT.at[p], KY.at[p], KX.at[p], RT.at[p], GH.at[p])
+        return carry
+
+    lax.fori_loop(0, SLOT_DEV, opening, 0)
+    wait_all(SEND1, RECV1, s1, r1)
+
+    def average_copy(pair, o):
+        return pltpu.make_async_remote_copy(
+            src_ref=PAIR.at[pair],
+            dst_ref=RECVA.at[pair, o],
+            send_sem=sa.at[pair, o],
+            recv_sem=ra.at[pair, o],
             device_id={"af": lax.rem(af + o, N_AF)},
             device_id_type=MESH,
         )
 
-    def begin(o, carry):
-        copy(o).start()
-        return carry
+    def one_patch(p, carry):
+        old = ST[0, p]
+        change = (total_of(RECV1, p) - old) * (1.0 / RATIO)
+        ghost_tiles(old + change, GH.at[p])
+        substep(B.at[p], A.at[p], HZ.at[p], HX.at[p], HY.at[p], HT.at[p], KY.at[p], KX.at[p], RT.at[p], GH.at[p])
+        ghost_tiles(old + 2.0 * change, GH.at[p])
+        substep(A.at[p], B.at[p], HZ.at[p], HX.at[p], HY.at[p], HT.at[p], KY.at[p], KX.at[p], RT.at[p], GH.at[p])
+        ghost_tiles(old + 3.0 * change, GH.at[p])
+        substep(B.at[p], A.at[p], HZ.at[p], HX.at[p], HY.at[p], HT.at[p], KY.at[p], KX.at[p], RT.at[p], GH.at[p])
+        for t in range(TILES):
+            for s in range(3):
+                for j in range(RATIO):
+                    result[p, s, t, pl.ds(j, 8, stride=4), :] = A[p, s, j + 1, :, pl.ds(t * 128, 128)]
+        for copy in store_patch(result, fine_out, p, sem_out):
+            copy.start()
+        value = patch_average(A.at[p])
+        for s in range(3):
+            AVG[p, s] = value[s * 8 : s * 8 + 8]
+        return carry
+
+    def two_patches(pair, carry):
+        lax.fori_loop(2 * pair, 2 * pair + 2, one_patch, 0)
+        for s in range(3):
+            both = jnp.where(lanes() < 64, AVG[2 * pair, s], rot(AVG[2 * pair + 1, s], 64))
+            PAIR[pair, s] = both
+            RECVA[pair, 0, s] = both
+
+        def begin(o, inner):
+            average_copy(pair, o).start()
+            return inner
+
+        lax.fori_loop(1, N_AF, begin, 0)
+        return carry
+
+    lax.fori_loop(0, 2, two_patches, 0)
+    down.wait()
+    up.wait()
+    lane = lanes()
+    change_low = edge_change(E[0], E[2], (col > 0).astype(jnp.float32))
+    change_high = edge_change(E[1], E[3], (col < N_COL - 1).astype(jnp.float32))
+    for s in range(3):
+        for x in range(16):
+            i = s * 16 + x
+            N[s, x + 1, :, 0:128] += jnp.where(lane == 0, rot(change_low, -i), 0.0)
+            N[s, x + 1, :, 128:256] += jnp.where(lane == 127, rot(change_high, 127 - i), 0.0)
 
     def finish(o, carry):
-        copy(o).wait_send()
-        copy(o).wait_recv()
-        return carry
-
-    lax.fori_loop(1, N_AF, begin, 0)
+        for pair in range(2):
+            average_copy(pair, o).wait_send()
+            average_copy(pair, o).wait_recv()
+        return carry
+
     lax.fori_loop(1, N_AF, finish, 0)
-    place_averages(cover, RECV, cnew, T)
+    place_averages(cover, RECVA, N, T)
     for s in range(3):
-        out[s] = jnp.transpose(T[s], (1, 0, 2))
-
-
-def averages_to_coarse(avg, cnew, cover):
-    f32 = jnp.float32
-    vmem = pl.BlockSpec(memory_space=pltpu.VMEM)
-    return pl.pallas_call(
-        average_kernel,
-        out_shape=jax.ShapeDtypeStruct((3, NZC, 16, 256), f32),
-        in_specs=[vmem, vmem, pl.BlockSpec(memory_space=pltpu.SMEM)],
-        out_specs=vmem,
-        scratch_shapes=[
-            pltpu.VMEM((3, 16, 8, 256), f32),
-            pltpu.VMEM((N_AF * 2, 3, 8, 128), f32),
-            pltpu.SemaphoreType.DMA((N_AF,)),
-            pltpu.SemaphoreType.DMA((N_AF,)),
-        ],
-        compiler_params=pltpu.CompilerParams(
-            collective_id=1, has_side_effects=True, vmem_limit_bytes=32 * 1024 * 1024
-        ),
-    )(avg, cnew, cover)
+        coarse_out[s] = jnp.transpose(T[s], (1, 0, 2))
+
+    def end_store(p, carry):
+        for copy in store_patch(result, fine_out, p, sem_out):
+            copy.wait()
+        return carry
+
+    lax.fori_loop(0, SLOT_DEV, end_store, 0)
 
 
 def per_device(
     coarse_state, coarse_kappa, coarse_rate, fine_state, fine_kappa, fine_rate, boxes, cover
 ):
-    strips, cnew = coarse(coarse_state, coarse_kappa, coarse_rate, boxes.T)
-    fields, avg = fine(fine_state, fine_kappa, fine_rate, strips)
-    return averages_to_coarse(avg, cnew, cover), fields
+    f32 = jnp.float32
+    hbm = pl.BlockSpec(memory_space=pl.ANY)
+    vmem = pl.BlockSpec(memory_space=pltpu.VMEM)
+    D = SLOT_DEV
+    message = pltpu.VMEM((N_AF, D, 8, 128), f32)
+    sems = pltpu.SemaphoreType.DMA
+    return pl.pallas_call(
+        kernel,
+        out_shape=(
+            jax.ShapeDtypeStruct((3, NZC, 16, 256), f32),
+            jax.ShapeDtypeStruct((D, 3, FZ, FXY), f32),
+        ),
+        in_specs=[hbm] * 8,
+        out_specs=(vmem, hbm),
+        scratch_shapes=[
+            pltpu.SMEM((2, 512), jnp.int32),
+            pltpu.SMEM((64, 128), jnp.int32),
+            pltpu.VMEM((5, 8, 16, 256), f32),
+            pltpu.VMEM((5, 20, 8, 256), f32),
+            pltpu.VMEM((3, 18, 8, 256), f32),
+            pltpu.VMEM((3, 16, 8, 256), f32),
+            pltpu.VMEM((4, 8, 128), f32),
+            pltpu.VMEM((65, 8, 128), f32),
+            message,
+            message,
+            message,
+            message,
+            pltpu.VMEM((2, 3, 8, 128), f32),
+            pltpu.VMEM((D, 3, 8, 128), f32),
+            pltpu.VMEM((2, N_AF, 3, 8, 128), f32),
+            pltpu.VMEM((D, 3, TILES, FZ, 128), f32),
+            pltpu.VMEM((D, TILES, FZ, 128), f32),
+            pltpu.VMEM((D, TILES, FZ, 128), f32),
+            pltpu.VMEM((D, 3, TILES, FZ, 128), f32),
+            pltpu.VMEM((D, 3, RATIO + 2, 8, FXY), f32),
+            pltpu.VMEM((D, 3, RATIO + 2, 8, FXY), f32),
+            pltpu.VMEM((D, RATIO + 1, 8, FXY), f32),
+            pltpu.VMEM((D, RATIO, 2, 8, FXY), f32),
+            pltpu.VMEM((D, RATIO, 2, 8, FXY), f32),
+            pltpu.VMEM((D, RATIO, 8, FXY), f32),
+            pltpu.VMEM((D, RATIO, 8, FXY), f32),
+            pltpu.VMEM((D, RATIO, 2, 8, 128), f32),
+            pltpu.VMEM((D, RATIO, 8, FXY), f32),
+            pltpu.VMEM((D, 3, TILES + 1, 8, 128), f32),
+            pltpu.VMEM((2, D, 8, 128), f32),
+            sems((5,)),
+            sems((2, 4)),
+            sems((N_AF,)),
+            sems((N_AF,)),
+            sems((N_AF,)),
+            sems((N_AF,)),
+            sems((2, N_AF)),
+            sems((2, N_AF)),
+            sems((D,)),
+            sems((D,)),
+        ],
+        compiler_params=pltpu.CompilerParams(
+            collective_id=0, has_side_effects=True, vmem_limit_bytes=60 * 1024 * 1024
+        ),
+    )(coarse_state, coarse_kappa, coarse_rate, fine_state, fine_kappa, fine_rate, boxes.T, cover)
 
 
 def solution(mesh):

time: 79.5 us -> 57.3 us (0.72); the launches traced: 78.3 us -> 57 us
  Pallas kernels: 69.9 us -> 51.9 us
  local copies, waits for them, and re-layouts: 7.72 us -> 4.49 us
    pallas_call x3 -> x1, Pallas kernels: 69.9 us -> 51.9 us  [per_device(): pl.pallas_call(kernel, out_shape=(jax.ShapeDtypeStruct((3, NZC, 16, 256),...]
    unnamed x17 -> x2, local copies, waits for them, and re-layouts: 7.72 us -> 4.49 us
where the time goes in v3:
time: 57.3 us; the launch traced here: 57 us
  Pallas kernels  51.9 us (91%)
  local copies, waits for them, and re-layouts  4.49 us (8%)
  between operations  0.64 us (1%)
    pallas_call x1, Pallas kernels, per_device(): pl.pallas_call(kernel, out_shape=(jax.ShapeDtypeStruct((3, NZC, 16, 256),...  51.9 us
    unnamed x2, local copies, waits for them, and re-layouts  4.49 us

profile of v3, /device:TPU:0, one launch (start us, length us, event | category | flops | bytes accessed | tf_op | source)
XLA Modules:
  0.0 57.0 jit_solution(9016124599684889830)
XLA Ops:
  0.6 51.9 %shard_map.95 = (f32[3,8,16,256]{3,2,1,0:T(8,128)}, f32[4,3,32,1024]{3,2,1,0:T(8,128)}) custom-call(f32[3,8,16,256]{3,2,1,0:T(8,128)} %cs.1, f32[8,16,256]{2,1,0:T(8,128)} %ck.1, f32[8,16,256]{2,1,0:T(8,128)} %cr.1, f32[4,3,32,1024]{3,2,1,0:T(8,128)} %fs.1, f32[4,32,1024]{2,1,0:T(8,128)} %fk.1, f32[4,32,1024]{2,1,0:T(8,128)} %fr.1, s32[2,512]{1,0:T(2,128)} %bitcast.1, ...), custom_call_target="tpu_custom_call" | custom-call | tf_op jit(solution)/shard_map/pallas_call | solution.py:529
  52.5 1.8 %copy.12 = f32[3,8,16,256]{3,2,1,0:T(8,128)} copy(f32[3,8,16,256]{3,2,1,0:T(8,128)} %get-tuple-element.4) | data formatting | bytes 786432
  54.3 2.7 %copy.13 = f32[4,3,32,1024]{3,2,1,0:T(8,128)} copy(f32[4,3,32,1024]{3,2,1,0:T(8,128)} %get-tuple-element.5) | data formatting | bytes 3145728

commit v4 on v3

--- a/solution.py
+++ b/solution.py
@@ -156,10 +156,13 @@
         plane(j, 0)
 
 
-def patch_average(A):
+def average_weights(W):
     rows = lax.broadcasted_iota(jnp.int32, (FXY, 128), 0)
     cols = lax.broadcasted_iota(jnp.int32, (FXY, 128), 1)
-    weights = jnp.where(cols == (rows // 128) * 8 + (rows % 32) // 4, 1.0 / 64.0, 0.0).astype(jnp.bfloat16)
+    W[...] = jnp.where(cols == (rows // 128) * 8 + (rows % 32) // 4, 1.0 / 64.0, 0.0).astype(jnp.bfloat16)
+
+
+def patch_average(A, W):
     sums = [
         (A[s, 1] + A[s, 2]) + (A[s, 3] + A[s, 4]) for s in range(3)
     ]
@@ -168,10 +171,8 @@
     rest = value - high.astype(jnp.float32)
     mid = rest.astype(jnp.bfloat16)
     low = (rest - mid.astype(jnp.float32)).astype(jnp.bfloat16)
-    out = jnp.zeros((24, 128), jnp.float32)
-    for part in (low, mid, high):
-        out = out + jnp.dot(part, weights, preferred_element_type=jnp.float32)
-    return out
+    out = jnp.dot(jnp.concatenate([low, mid, high], axis=0), W[...], preferred_element_type=jnp.float32)
+    return out[0:24] + out[24:48] + out[48:72]
 
 
 MESH = pl.DeviceIdType.MESH
@@ -211,22 +212,20 @@
     return rows
 
 
-def pack_strips(P, base, B):
-    lane = lanes((8, 256))
-    within = lane % 8
+def pack_strips(P, B):
+    within = lanes((8, 256)) % 8
     for bx in range(2):
+        sides = []
+        for s in range(3):
+            sides.append(P[s, 15 if bx == 0 else 7])
+            sides.append(P[s, 8 if bx == 0 else 0])
+            for turn in (1, -BLK):
+                side = rot(P[s, BLK * bx], turn)
+                for a in range(1, BLK):
+                    side = jnp.where(within == a, rot(P[s, BLK * bx + a], a + turn), side)
+                sides.append(side)
         for half in range(2):
-            cut = pl.ds(half * 128, 128)
-            rows = []
-            for s in range(3):
-                rows.append(P[s, base + BLK * bx - 1, :, cut])
-                rows.append(P[s, base + BLK * bx + BLK, :, cut])
-                for turn in (1, -BLK):
-                    side = jnp.zeros((8, 128), jnp.float32)
-                    for a in range(BLK):
-                        moved = rot(P[s, base + BLK * bx + a], a + turn)[:, half * 128 : half * 128 + 128]
-                        side = jnp.where(within[:, :128] == a, moved, side)
-                    rows.append(side)
+            rows = [side[:, half * 128 : half * 128 + 128] for side in sides]
             rows += rows[:4]
             for g, row in enumerate(swap_groups(rows, (8, 4, 2, 1))):
                 B[bx * 32 + half * 16 + g] = row
@@ -239,8 +238,8 @@
     for q in range(4):
         for x in range(16):
             i = q * 16 + x
-            low = jnp.where(lane == i, rot(C[q, x + 2, :, 0:128], i), low)
-            high = jnp.where(lane == i, rot(C[q, x + 2, :, 128:256], i + 1), high)
+            low = jnp.where(lane == i, rot(C[q, x + 1, :, 0:128], i), low)
+            high = jnp.where(lane == i, rot(C[q, x + 1, :, 128:256], i + 1), high)
     E[0] = low
     E[1] = high
 
@@ -260,50 +259,88 @@
     lane = lanes((8, 256))
     sub = lax.broadcasted_iota(jnp.int32, (8, 256), 0)
     before = safe_face(C[3, 0], C[3, 1])
-    for xi in range(1, 19):
-        k = C[3, xi]
-        rate = C[4, xi] * DT_COARSE
-        after = safe_face(k, C[3, xi + 1])
+    for x in range(16):
+        k = C[3, x + 1]
+        rate = C[4, x + 1] * DT_COARSE
+        after = safe_face(k, C[3, x + 2])
         hzu = jnp.where(sub == 7, 0.0, safe_face(k, pltpu.roll(k, 7, 0)))
         hzd = jnp.where(sub == 0, 0.0, pltpu.roll(hzu, 1, 0))
         hyu = jnp.where(lane == 255, 0.0, safe_face(k, rot(k, -1)))
         hyd = jnp.where(lane == 0, 0.0, rot(hyu, 1))
         total = (hzu + hzd) + (before + after) + (hyu + hyd)
-        us = [C[s, xi] for s in range(3)]
+        us = [C[s, x + 1] for s in range(3)]
         react = rate * (us[0] * us[1] - us[2])
         for s in range(3):
             u = us[s]
             flow = (hzu * pltpu.roll(u, 7, 0) + hzd * pltpu.roll(u, 1, 0)) + (
-                after * C[s, xi + 1] + before * C[s, xi - 1]
+                after * C[s, x + 2] + before * C[s, x]
             )
             flow = flow + (hyu * rot(u, -1) + hyd * rot(u, 1)) - total * u
             if s > 0:
                 flow = DIFFUSE[s] * flow
-            N[s, xi - 1] = u + (flow - react if s < 2 else flow + react)
+            N[s, x] = u + (flow - react if s < 2 else flow + react)
         before = after
 
 
-def block_row(boxes, af, col, p):
-    at = col * (N_AF * SLOT_DEV) + p
-    x = boxes[0, at] - af * 2
-    y = boxes[1, at] - col * 32
-    return jnp.where((x >= 0) & (x < 2), jnp.clip(x * 32 + y, 0, 63), 64)
-
-
-def send_strips(boxes, B, SEND, RECV, send_sem, recv_sem):
+def strip_tables(boxes, ROW, WHICH, MASK):
     af = lax.axis_index("af")
     col = lax.axis_index("col")
+
+    def one(p, carry):
+        at = col * (N_AF * SLOT_DEV) + p
+        x = boxes[0, at] - af * 2 + 1
+        y = boxes[1, at] - col * 32
+        near = (x >= 0) & (x < 4)
+        column = jnp.where((x == 1) | (x == 3), 0, 32)
+        ROW[p] = jnp.clip(column + y, 0, 63)
+        WHICH[p] = jnp.where(near, x, 4)
+        return carry
+
+    lax.fori_loop(0, N_AF * SLOT_DEV, one, 0)
+    lane = lanes()
+    side = (lane // 8) % 4
+    used = lane < 96
+    MASK[0] = jnp.where(used & (side == 1), 1.0, 0.0)
+    MASK[1] = jnp.where(used & (side != 0), 1.0, 0.0)
+    MASK[2] = jnp.where(used & (side != 1), 1.0, 0.0)
+    MASK[3] = jnp.where(used & (side == 0), 1.0, 0.0)
+    MASK[4] = jnp.zeros((8, 128), jnp.float32)
+
+
+def fill_message(d, B, ROW, WHICH, MASK, OUT):
+    lane = lanes()
+    rows = []
     for j in range(SLOT_DEV):
-        RECV[0, j] = B[block_row(boxes, af, col, af * SLOT_DEV + j)]
+        p = d * SLOT_DEV + j
+        rows.append(rot(B[ROW[p]] * MASK[WHICH[p]], 96 * j))
+    OUT[0] = jnp.where(lane < 96, rows[0], rows[1])
+    OUT[1] = jnp.where(lane < 64, rows[1], rows[2])
+    OUT[2] = jnp.where(lane < 32, rows[2], rows[3])
+
+
+def fill_messages(B, ROW, WHICH, MASK, SEND, RECV, then):
+    af = lax.axis_index("af")
+    fill_message(af, B, ROW, WHICH, MASK, RECV.at[0])
 
     def one(o, carry):
-        d = lax.rem(af + o, N_AF)
-        for j in range(SLOT_DEV):
-            SEND[o, j] = B[block_row(boxes, af, col, d * SLOT_DEV + j)]
-        spread_copy(o, d, SEND, RECV, send_sem, recv_sem).start()
+        fill_message(lax.rem(af + o, N_AF), B, ROW, WHICH, MASK, SEND.at[o])
+        then(o)
         return carry
 
     lax.fori_loop(1, N_AF, one, 0)
+
+
+def sum_messages(RECV, ST):
+    lane = lanes()
+
+    def one(o, totals):
+        return tuple(totals[i] + RECV[o, i] for i in range(3))
+
+    a, b, c = lax.fori_loop(1, N_AF, one, (RECV[0, 0], RECV[0, 1], RECV[0, 2]))
+    ST[0] = a
+    ST[1] = rot(jnp.where(lane >= 96, a, b), -96)
+    ST[2] = rot(jnp.where(lane >= 64, b, c), -64)
+    ST[3] = rot(c, -32)
 
 
 def spread_copy(o, d, SEND, RECV, send_sem, recv_sem):
@@ -317,58 +354,64 @@
     )
 
 
-def wait_all(SEND, RECV, send_sem, recv_sem):
+def wait_messages(SEND, RECV, send_sem, recv_sem, received):
     af = lax.axis_index("af")
 
     def one(o, carry):
         copy = spread_copy(o, lax.rem(af + o, N_AF), SEND, RECV, send_sem, recv_sem)
-        copy.wait_send()
-        copy.wait_recv()
+        if received:
+            copy.wait_recv()
+        else:
+            copy.wait_send()
         return carry
 
     lax.fori_loop(1, N_AF, one, 0)
 
 
-def place_averages(cover, RECV, cnew, T):
+def place_tables(cover, PAIR_AT, FROM_AT, ODD, COVERED):
     af = lax.axis_index("af")
     col = lax.axis_index("col")
-    lane = lanes()
-    group = lane // 8
+    group = lanes() // 8
     for lx in range(2):
         for h in range(2):
             own = jnp.full((8, 128), -1, jnp.int32)
-            where_at = []
             for g in range(16):
                 p = cover[af * 2 + lx, col * 32 + h * 16 + g]
                 own = jnp.where(group == g, p, own)
-                q = jnp.maximum(p - col * (N_AF * SLOT_DEV), 0)
+                q = jnp.clip(p - col * (N_AF * SLOT_DEV), 0, N_AF * SLOT_DEV - 1)
                 source = lax.div(q, SLOT_DEV)
                 slot = lax.rem(q, SLOT_DEV)
-                at = (lax.div(slot, 2), lax.rem(af + N_AF - source, N_AF))
-                where_at.append((at, lax.rem(slot, 2)))
-            covered = own >= 0
+                at = (lx * 2 + h) * 16 + g
+                PAIR_AT[at] = lax.div(slot, 2)
+                FROM_AT[at] = lax.rem(af + N_AF - source, N_AF)
+                ODD[at] = lax.rem(slot, 2)
+            COVERED[lx * 2 + h] = jnp.where(own >= 0, 1.0, 0.0)
+
+
+def place_averages(PAIR_AT, FROM_AT, ODD, COVERED, RECV, N, T):
+    lane = lanes()
+    for lx in range(2):
+        for h in range(2):
+            covered = COVERED[lx * 2 + h] > 0.0
+            cut = pl.ds(h * 128, 128)
             for s in range(3):
                 rows = []
                 for g in range(8):
-                    at, odd = where_at[g]
-                    first = RECV[at[0], at[1], s]
-                    first = jnp.where(odd == 1, rot(first, 64), first)
-                    at, odd = where_at[g + 8]
-                    second = RECV[at[0], at[1], s]
-                    second = jnp.where(odd == 1, second, rot(second, 64))
+                    at = (lx * 2 + h) * 16 + g
+                    first = RECV[PAIR_AT[at], FROM_AT[at], s]
+                    first = jnp.where(ODD[at] == 1, rot(first, 64), first)
+                    at = at + 8
+                    second = RECV[PAIR_AT[at], FROM_AT[at], s]
+                    second = jnp.where(ODD[at] == 1, second, rot(second, 64))
                     rows.append(jnp.where(lane < 64, first, second))
                 for x, row in enumerate(swap_groups(rows, (4, 2, 1))):
-                    cut = pl.ds(h * 128, 128)
-                    T[s, lx * BLK + x, :, cut] = jnp.where(covered, row, cnew[s, lx * BLK + x + 1, :, cut])
-
-
-def total_of(RECV, j):
-    return lax.fori_loop(1, N_AF, lambda o, total: total + RECV[o, j], RECV[0, j])
+                    T[s, lx * BLK + x, :, cut] = jnp.where(covered, row, N[s, lx * BLK + x, :, cut])
 
 
 def kernel(
     cs, ck, cr, fs, fk, fr, boxes_in, cover_in, coarse_out, fine_out,
-    boxes, cover, CI, C, N, T, E, BLOCKS, SEND0, SEND1, RECV0, RECV1, PAIR, AVG, RECVA,
+    boxes, cover, ROW, WHICH, PAIR_AT, FROM_AT, ODD, MASK, COVERED, W,
+    CI, C, N, T, E, BLOCKS, SEND0, SEND1, RECV0, RECV1, PAIR, AVG, RECVA,
     stage_u, stage_k, stage_r, result, A, B, HZ, HX, HY, HT, KY, KX, RT, GH, ST,
     load_sem, halo_sem, s0, r0, s1, r1, sa, ra, sem_in, sem_out,
 ):
@@ -395,7 +438,11 @@
     for copy in first:
         copy.wait()
     for q in range(5):
-        C[q, 2:18] = jnp.transpose(CI[q], (1, 0, 2))
+        C[q, 1:17] = jnp.transpose(CI[q], (1, 0, 2))
+    pack_edges(C, E)
+    strip_tables(boxes, ROW, WHICH, MASK)
+    pack_strips(C.at[:, 1:17], BLOCKS)
+    fill_messages(BLOCKS, ROW, WHICH, MASK, SEND0, RECV0, lambda o: None)
     pl.semaphore_wait(barrier, N_AF + 1)
 
     def halo(src, dst, sem, where):
@@ -404,25 +451,20 @@
             device_id=where, device_id_type=MESH,
         )
 
-    right = halo(C.at[:, 16:18], C.at[:, 0:2], 0, {"af": lax.rem(af + 1, N_AF)})
-    left = halo(C.at[:, 2:4], C.at[:, 18:20], 1, {"af": lax.rem(af + N_AF - 1, N_AF)})
+    right = halo(C.at[0:4, 16], C.at[0:4, 0], 0, {"af": lax.rem(af + 1, N_AF)})
+    left = halo(C.at[0:4, 1], C.at[0:4, 17], 1, {"af": lax.rem(af + N_AF - 1, N_AF)})
     right.start()
     left.start()
-    pack_edges(C, E)
+
+    def begin_old(o, carry):
+        spread_copy(o, lax.rem(af + o, N_AF), SEND0, RECV0, s0, r0).start()
+        return carry
+
+    lax.fori_loop(1, N_AF, begin_old, 0)
     down = halo(E.at[0], E.at[3], 2, {"col": lax.rem(col + N_COL - 1, N_COL)})
     up = halo(E.at[1], E.at[2], 3, {"col": lax.rem(col + 1, N_COL)})
     down.start()
     up.start()
-    BLOCKS[64] = jnp.zeros((8, 128), jnp.float32)
-    right.wait()
-    left.wait()
-    C[3, 0:2] = C[3, 0:2] * (af > 0).astype(jnp.float32)
-    C[3, 18:20] = C[3, 18:20] * (af < N_AF - 1).astype(jnp.float32)
-    pack_strips(C, 2, BLOCKS)
-    send_strips(boxes, BLOCKS, SEND0, RECV0, s0, r0)
-    coarse_update(C, N)
-    pack_strips(N, 1, BLOCKS)
-    send_strips(boxes, BLOCKS, SEND1, RECV1, s1, r1)
 
     def prepare(p, carry):
         for copy in load_patch(fs, fk, fr, p, stage_u, stage_k, stage_r, sem_in):
@@ -430,17 +472,30 @@
         patch_setup(p, stage_u, stage_k, stage_r, A.at[p], HZ.at[p], HX.at[p], HY.at[p], HT.at[p], KY.at[p], KX.at[p], RT.at[p])
         return carry
 
-    lax.fori_loop(0, SLOT_DEV, prepare, 0)
-    wait_all(SEND0, RECV0, s0, r0)
+    lax.fori_loop(0, 2, prepare, 0)
+    right.wait()
+    left.wait()
+    C[3, 0] = C[3, 0] * (af > 0).astype(jnp.float32)
+    C[3, 17] = C[3, 17] * (af < N_AF - 1).astype(jnp.float32)
+    coarse_update(C, N)
+    pack_strips(N, BLOCKS)
+    fill_messages(
+        BLOCKS, ROW, WHICH, MASK, SEND1, RECV1,
+        lambda o: spread_copy(o, lax.rem(af + o, N_AF), SEND1, RECV1, s1, r1).start(),
+    )
+    lax.fori_loop(2, SLOT_DEV, prepare, 0)
+    average_weights(W)
+    wait_messages(SEND0, RECV0, s0, r0, True)
+    sum_messages(RECV0, ST.at[0])
 
     def opening(p, carry):
-        ST[0, p] = total_of(RECV0, p)
         ghost_tiles(ST[0, p], GH.at[p])
         substep(A.at[p], B.at[p], HZ.at[p], HX.at[p], HY.at[p], HT.at[p], KY.at[p], KX.at[p], RT.at[p], GH.at[p])
         return carry
 
     lax.fori_loop(0, SLOT_DEV, opening, 0)
-    wait_all(SEND1, RECV1, s1, r1)
+    wait_messages(SEND1, RECV1, s1, r1, True)
+    sum_messages(RECV1, ST.at[1])
 
     def average_copy(pair, o):
         return pltpu.make_async_remote_copy(
@@ -454,22 +509,25 @@
 
     def one_patch(p, carry):
         old = ST[0, p]
-        change = (total_of(RECV1, p) - old) * (1.0 / RATIO)
+        change = (ST[1, p] - old) * (1.0 / RATIO)
         ghost_tiles(old + change, GH.at[p])
         substep(B.at[p], A.at[p], HZ.at[p], HX.at[p], HY.at[p], HT.at[p], KY.at[p], KX.at[p], RT.at[p], GH.at[p])
         ghost_tiles(old + 2.0 * change, GH.at[p])
         substep(A.at[p], B.at[p], HZ.at[p], HX.at[p], HY.at[p], HT.at[p], KY.at[p], KX.at[p], RT.at[p], GH.at[p])
         ghost_tiles(old + 3.0 * change, GH.at[p])
         substep(B.at[p], A.at[p], HZ.at[p], HX.at[p], HY.at[p], HT.at[p], KY.at[p], KX.at[p], RT.at[p], GH.at[p])
+        value = patch_average(A.at[p], W)
+        for s in range(3):
+            AVG[p, s] = value[s * 8 : s * 8 + 8]
+        return carry
+
+    def write_patch(p, carry):
         for t in range(TILES):
             for s in range(3):
                 for j in range(RATIO):
                     result[p, s, t, pl.ds(j, 8, stride=4), :] = A[p, s, j + 1, :, pl.ds(t * 128, 128)]
         for copy in store_patch(result, fine_out, p, sem_out):
             copy.start()
-        value = patch_average(A.at[p])
-        for s in range(3):
-            AVG[p, s] = value[s * 8 : s * 8 + 8]
         return carry
 
     def two_patches(pair, carry):
@@ -487,6 +545,7 @@
         return carry
 
     lax.fori_loop(0, 2, two_patches, 0)
+    lax.fori_loop(0, SLOT_DEV, write_patch, 0)
     down.wait()
     up.wait()
     lane = lanes()
@@ -495,8 +554,11 @@
     for s in range(3):
         for x in range(16):
             i = s * 16 + x
-            N[s, x + 1, :, 0:128] += jnp.where(lane == 0, rot(change_low, -i), 0.0)
-            N[s, x + 1, :, 128:256] += jnp.where(lane == 127, rot(change_high, 127 - i), 0.0)
+            N[s, x, :, 0:128] += jnp.where(lane == 0, rot(change_low, -i), 0.0)
+            N[s, x, :, 128:256] += jnp.where(lane == 127, rot(change_high, 127 - i), 0.0)
+    place_tables(cover, PAIR_AT, FROM_AT, ODD, COVERED)
+    wait_messages(SEND0, RECV0, s0, r0, False)
+    wait_messages(SEND1, RECV1, s1, r1, False)
 
     def finish(o, carry):
         for pair in range(2):
@@ -505,7 +567,7 @@
         return carry
 
     lax.fori_loop(1, N_AF, finish, 0)
-    place_averages(cover, RECVA, N, T)
+    place_averages(PAIR_AT, FROM_AT, ODD, COVERED, RECVA, N, T)
     for s in range(3):
         coarse_out[s] = jnp.transpose(T[s], (1, 0, 2))
 
@@ -524,25 +586,34 @@
     hbm = pl.BlockSpec(memory_space=pl.ANY)
     vmem = pl.BlockSpec(memory_space=pltpu.VMEM)
     D = SLOT_DEV
-    message = pltpu.VMEM((N_AF, D, 8, 128), f32)
+    message = pltpu.VMEM((N_AF, 3, 8, 128), f32)
+    table = pltpu.SMEM((128,), jnp.int32)
     sems = pltpu.SemaphoreType.DMA
     return pl.pallas_call(
         kernel,
         out_shape=(
-            jax.ShapeDtypeStruct((3, NZC, 16, 256), f32),
-            jax.ShapeDtypeStruct((D, 3, FZ, FXY), f32),
+            pltpu.VMEM((3, NZC, 16, 256), f32),
+            pltpu.VMEM((D, 3, FZ, FXY), f32),
         ),
         in_specs=[hbm] * 8,
-        out_specs=(vmem, hbm),
+        out_specs=(vmem, vmem),
         scratch_shapes=[
             pltpu.SMEM((2, 512), jnp.int32),
             pltpu.SMEM((64, 128), jnp.int32),
+            table,
+            table,
+            table,
+            table,
+            table,
+            pltpu.VMEM((5, 8, 128), f32),
+            pltpu.VMEM((4, 8, 128), f32),
+            pltpu.VMEM((FXY, 128), jnp.bfloat16),
             pltpu.VMEM((5, 8, 16, 256), f32),
-            pltpu.VMEM((5, 20, 8, 256), f32),
-            pltpu.VMEM((3, 18, 8, 256), f32),
+            pltpu.VMEM((5, 18, 8, 256), f32),
+            pltpu.VMEM((3, 16, 8, 256), f32),
             pltpu.VMEM((3, 16, 8, 256), f32),
             pltpu.VMEM((4, 8, 128), f32),
-            pltpu.VMEM((65, 8, 128), f32),
+            pltpu.VMEM((64, 8, 128), f32),
             message,
             message,
             message,
@@ -579,7 +650,12 @@
         compiler_params=pltpu.CompilerParams(
             collective_id=0, has_side_effects=True, vmem_limit_bytes=60 * 1024 * 1024
         ),
-    )(coarse_state, coarse_kappa, coarse_rate, fine_state, fine_kappa, fine_rate, boxes.T, cover)
+    )(
+        *[
+            pltpu.with_memory_space_constraint(x, pltpu.HBM)
+            for x in (coarse_state, coarse_kappa, coarse_rate, fine_state, fine_kappa, fine_rate, boxes.T, cover)
+        ]
+    )
 
 
 def solution(mesh):

time: 57.3 us -> 48 us (0.84)
  Pallas kernels: 51.9 us -> 45.3 us
  local copies, waits for them, and re-layouts: 4.49 us -> 1.89 us
    pallas_call x1, Pallas kernels: 51.9 us -> 45.3 us  [per_device(): pl.pallas_call(kernel, out_shape=(pltpu.VMEM((3, NZC, 16, 256), f32), plt...]
    unnamed x2, local copies, waits for them, and re-layouts: 4.49 us -> 1.89 us
where the time goes in v4:
time: 48 us; the launch traced here: 47.9 us
  Pallas kernels  45.3 us (94%)
  local copies, waits for them, and re-layouts  1.89 us (4%)
  between operations  0.64 us (1%)
    pallas_call x1, Pallas kernels, per_device(): pl.pallas_call(kernel, out_shape=(pltpu.VMEM((3, NZC, 16, 256), f32), plt...  45.3 us
    unnamed x2, local copies, waits for them, and re-layouts  1.89 us

profile of v4, /device:TPU:0, one launch (start us, length us, event | category | flops | bytes accessed | tf_op | source)
XLA Modules:
  0.0 47.9 jit_solution(4810551964750544703)
XLA Ops:
  0.6 45.3 %shard_map.95 = (f32[3,8,16,256]{3,2,1,0:T(8,128)S(1)}, f32[4,3,32,1024]{3,2,1,0:T(8,128)S(1)}) custom-call(f32[3,8,16,256]{3,2,1,0:T(8,128)} %cs.1, f32[8,16,256]{2,1,0:T(8,128)} %ck.1, f32[8,16,256]{2,1,0:T(8,128)} %cr.1, f32[4,3,32,1024]{3,2,1,0:T(8,128)} %fs.1, f32[4,32,1024]{2,1,0:T(8,128)} %fk.1, f32[4,32,1024]{2,1,0:T(8,128)} %fr.1, ...), custom_call_target="tpu_custom_call" | custom-call | tf_op jit(solution)/shard_map/pallas_call | solution.py:592
  46.0 0.7 %copy.12 = f32[3,8,16,256]{3,2,1,0:T(8,128)} copy(f32[3,8,16,256]{3,2,1,0:T(8,128)S(1)} %get-tuple-element.2) | data formatting | bytes 786432
  46.7 1.1 %copy.13 = f32[4,3,32,1024]{3,2,1,0:T(8,128)} copy(f32[4,3,32,1024]{3,2,1,0:T(8,128)S(1)} %get-tuple-element.3) | data formatting | bytes 3145728

commit v5 on v4

--- a/solution.py
+++ b/solution.py
@@ -286,17 +286,19 @@
     af = lax.axis_index("af")
     col = lax.axis_index("col")
 
-    def one(p, carry):
-        at = col * (N_AF * SLOT_DEV) + p
-        x = boxes[0, at] - af * 2 + 1
-        y = boxes[1, at] - col * 32
-        near = (x >= 0) & (x < 4)
-        column = jnp.where((x == 1) | (x == 3), 0, 32)
-        ROW[p] = jnp.clip(column + y, 0, 63)
-        WHICH[p] = jnp.where(near, x, 4)
-        return carry
-
-    lax.fori_loop(0, N_AF * SLOT_DEV, one, 0)
+    def eight(i, carry):
+        for q in range(8):
+            p = i * 8 + q
+            at = col * (N_AF * SLOT_DEV) + p
+            x = boxes[0, at] - af * 2 + 1
+            y = boxes[1, at] - col * 32
+            near = (x >= 0) & (x < 4)
+            column = jnp.where((x == 1) | (x == 3), 0, 32)
+            ROW[p] = jnp.clip(column + y, 0, 63)
+            WHICH[p] = jnp.where(near, x, 4)
+        return carry
+
+    lax.fori_loop(0, N_AF * SLOT_DEV // 8, eight, 0)
     lane = lanes()
     side = (lane // 8) % 4
     used = lane < 96
@@ -318,16 +320,24 @@
     OUT[2] = jnp.where(lane < 32, rows[2], rows[3])
 
 
-def fill_messages(B, ROW, WHICH, MASK, SEND, RECV, then):
+def fill_messages(B, ROW, WHICH, MASK, SEND, RECV, send_sem, recv_sem):
     af = lax.axis_index("af")
-    fill_message(af, B, ROW, WHICH, MASK, RECV.at[0])
-
-    def one(o, carry):
-        fill_message(lax.rem(af + o, N_AF), B, ROW, WHICH, MASK, SEND.at[o])
-        then(o)
-        return carry
-
-    lax.fori_loop(1, N_AF, one, 0)
+
+    def four(i, carry):
+        for q in range(4):
+            o = i * 4 + q
+            fill_message(lax.rem(af + o, N_AF), B, ROW, WHICH, MASK, SEND.at[o])
+        for q in range(4):
+            o = i * 4 + q
+
+            @pl.when(o > 0)
+            def start():
+                spread_copy(o, lax.rem(af + o, N_AF), SEND, RECV, send_sem, recv_sem).start()
+
+        return carry
+
+    lax.fori_loop(0, N_AF // 4, four, 0)
+    RECV[0] = SEND[0]
 
 
 def sum_messages(RECV, ST):
@@ -347,25 +357,28 @@
     return pltpu.make_async_remote_copy(
         src_ref=SEND.at[o],
         dst_ref=RECV.at[o],
-        send_sem=send_sem.at[o],
-        recv_sem=recv_sem.at[o],
+        send_sem=send_sem,
+        recv_sem=recv_sem,
         device_id={"af": d},
         device_id_type=MESH,
     )
 
 
-def wait_messages(SEND, RECV, send_sem, recv_sem, received):
+def wait_messages(RECV, send_sem, recv_sem, received):
     af = lax.axis_index("af")
-
-    def one(o, carry):
-        copy = spread_copy(o, lax.rem(af + o, N_AF), SEND, RECV, send_sem, recv_sem)
-        if received:
-            copy.wait_recv()
-        else:
-            copy.wait_send()
-        return carry
-
-    lax.fori_loop(1, N_AF, one, 0)
+    whole = RECV.at[pl.ds(1, N_AF - 1)]
+    copy = pltpu.make_async_remote_copy(
+        src_ref=whole,
+        dst_ref=whole,
+        send_sem=send_sem,
+        recv_sem=recv_sem,
+        device_id={"af": lax.rem(af + 1, N_AF)},
+        device_id_type=MESH,
+    )
+    if received:
+        copy.wait_recv()
+    else:
+        copy.wait_send()
 
 
 def place_tables(cover, PAIR_AT, FROM_AT, ODD, COVERED):
@@ -413,7 +426,7 @@
     boxes, cover, ROW, WHICH, PAIR_AT, FROM_AT, ODD, MASK, COVERED, W,
     CI, C, N, T, E, BLOCKS, SEND0, SEND1, RECV0, RECV1, PAIR, AVG, RECVA,
     stage_u, stage_k, stage_r, result, A, B, HZ, HX, HY, HT, KY, KX, RT, GH, ST,
-    load_sem, halo_sem, s0, r0, s1, r1, sa, ra, sem_in, sem_out,
+    load_sem, halo_sem, exchange, averaged, sem_in, sem_out,
 ):
     af = lax.axis_index("af")
     col = lax.axis_index("col")
@@ -439,10 +452,6 @@
         copy.wait()
     for q in range(5):
         C[q, 1:17] = jnp.transpose(CI[q], (1, 0, 2))
-    pack_edges(C, E)
-    strip_tables(boxes, ROW, WHICH, MASK)
-    pack_strips(C.at[:, 1:17], BLOCKS)
-    fill_messages(BLOCKS, ROW, WHICH, MASK, SEND0, RECV0, lambda o: None)
     pl.semaphore_wait(barrier, N_AF + 1)
 
     def halo(src, dst, sem, where):
@@ -456,15 +465,9 @@
     right.start()
     left.start()
 
-    def begin_old(o, carry):
-        spread_copy(o, lax.rem(af + o, N_AF), SEND0, RECV0, s0, r0).start()
-        return carry
-
-    lax.fori_loop(1, N_AF, begin_old, 0)
-    down = halo(E.at[0], E.at[3], 2, {"col": lax.rem(col + N_COL - 1, N_COL)})
-    up = halo(E.at[1], E.at[2], 3, {"col": lax.rem(col + 1, N_COL)})
-    down.start()
-    up.start()
+    strip_tables(boxes, ROW, WHICH, MASK)
+    pack_strips(C.at[:, 1:17], BLOCKS)
+    fill_messages(BLOCKS, ROW, WHICH, MASK, SEND0, RECV0, exchange.at[0], exchange.at[1])
 
     def prepare(p, carry):
         for copy in load_patch(fs, fk, fr, p, stage_u, stage_k, stage_r, sem_in):
@@ -472,20 +475,21 @@
         patch_setup(p, stage_u, stage_k, stage_r, A.at[p], HZ.at[p], HX.at[p], HY.at[p], HT.at[p], KY.at[p], KX.at[p], RT.at[p])
         return carry
 
-    lax.fori_loop(0, 2, prepare, 0)
     right.wait()
     left.wait()
     C[3, 0] = C[3, 0] * (af > 0).astype(jnp.float32)
     C[3, 17] = C[3, 17] * (af < N_AF - 1).astype(jnp.float32)
     coarse_update(C, N)
     pack_strips(N, BLOCKS)
-    fill_messages(
-        BLOCKS, ROW, WHICH, MASK, SEND1, RECV1,
-        lambda o: spread_copy(o, lax.rem(af + o, N_AF), SEND1, RECV1, s1, r1).start(),
-    )
-    lax.fori_loop(2, SLOT_DEV, prepare, 0)
+    fill_messages(BLOCKS, ROW, WHICH, MASK, SEND1, RECV1, exchange.at[2], exchange.at[3])
+    pack_edges(C, E)
+    down = halo(E.at[0], E.at[3], 2, {"col": lax.rem(col + N_COL - 1, N_COL)})
+    up = halo(E.at[1], E.at[2], 3, {"col": lax.rem(col + 1, N_COL)})
+    down.start()
+    up.start()
+    lax.fori_loop(0, SLOT_DEV, prepare, 0)
     average_weights(W)
-    wait_messages(SEND0, RECV0, s0, r0, True)
+    wait_messages(RECV0, exchange.at[0], exchange.at[1], True)
     sum_messages(RECV0, ST.at[0])
 
     def opening(p, carry):
@@ -494,15 +498,15 @@
         return carry
 
     lax.fori_loop(0, SLOT_DEV, opening, 0)
-    wait_messages(SEND1, RECV1, s1, r1, True)
+    wait_messages(RECV1, exchange.at[2], exchange.at[3], True)
     sum_messages(RECV1, ST.at[1])
 
     def average_copy(pair, o):
         return pltpu.make_async_remote_copy(
             src_ref=PAIR.at[pair],
             dst_ref=RECVA.at[pair, o],
-            send_sem=sa.at[pair, o],
-            recv_sem=ra.at[pair, o],
+            send_sem=averaged.at[0, pair],
+            recv_sem=averaged.at[1, pair],
             device_id={"af": lax.rem(af + o, N_AF)},
             device_id_type=MESH,
         )
@@ -537,11 +541,8 @@
             PAIR[pair, s] = both
             RECVA[pair, 0, s] = both
 
-        def begin(o, inner):
+        for o in range(1, N_AF):
             average_copy(pair, o).start()
-            return inner
-
-        lax.fori_loop(1, N_AF, begin, 0)
         return carry
 
     lax.fori_loop(0, 2, two_patches, 0)
@@ -557,16 +558,12 @@
             N[s, x, :, 0:128] += jnp.where(lane == 0, rot(change_low, -i), 0.0)
             N[s, x, :, 128:256] += jnp.where(lane == 127, rot(change_high, 127 - i), 0.0)
     place_tables(cover, PAIR_AT, FROM_AT, ODD, COVERED)
-    wait_messages(SEND0, RECV0, s0, r0, False)
-    wait_messages(SEND1, RECV1, s1, r1, False)
-
-    def finish(o, carry):
-        for pair in range(2):
-            average_copy(pair, o).wait_send()
-            average_copy(pair, o).wait_recv()
-        return carry
-
-    lax.fori_loop(1, N_AF, finish, 0)
+    wait_messages(RECV0, exchange.at[0], exchange.at[1], False)
+    wait_messages(RECV1, exchange.at[2], exchange.at[3], False)
+
+    for pair in range(2):
+        wait_messages(RECVA.at[pair], averaged.at[0, pair], averaged.at[1, pair], False)
+        wait_messages(RECVA.at[pair], averaged.at[0, pair], averaged.at[1, pair], True)
     place_averages(PAIR_AT, FROM_AT, ODD, COVERED, RECVA, N, T)
     for s in range(3):
         coarse_out[s] = jnp.transpose(T[s], (1, 0, 2))
@@ -638,12 +635,8 @@
             pltpu.VMEM((2, D, 8, 128), f32),
             sems((5,)),
             sems((2, 4)),
-            sems((N_AF,)),
-            sems((N_AF,)),
-            sems((N_AF,)),
-            sems((N_AF,)),
-            sems((2, N_AF)),
-            sems((2, N_AF)),
+            sems((4,)),
+            sems((2, 2)),
             sems((D,)),
             sems((D,)),
         ],

time: 48 us -> 41.5 us (0.86)
  Pallas kernels: 45.3 us -> 38.9 us
    pallas_call x1, Pallas kernels: 45.3 us -> 38.9 us  [per_device(): pl.pallas_call(kernel, out_shape=(pltpu.VMEM((3, NZC, 16, 256), f32), plt...]
where the time goes in v5:
time: 41.5 us; the launch traced here: 41.4 us
  Pallas kernels  38.9 us (94%)
  local copies, waits for them, and re-layouts  1.89 us (5%)
  between operations  0.64 us (2%)
    pallas_call x1, Pallas kernels, per_device(): pl.pallas_call(kernel, out_shape=(pltpu.VMEM((3, NZC, 16, 256), f32), plt...  38.9 us
    unnamed x2, local copies, waits for them, and re-layouts  1.89 us

profile of v5, /device:TPU:0, one launch (start us, length us, event | category | flops | bytes accessed | tf_op | source)
XLA Modules:
  0.0 41.4 jit_solution(17541379185481118792)
XLA Ops:
  0.6 38.9 %shard_map.95 = (f32[3,8,16,256]{3,2,1,0:T(8,128)S(1)}, f32[4,3,32,1024]{3,2,1,0:T(8,128)S(1)}) custom-call(f32[3,8,16,256]{3,2,1,0:T(8,128)} %cs.1, f32[8,16,256]{2,1,0:T(8,128)} %ck.1, f32[8,16,256]{2,1,0:T(8,128)} %cr.1, f32[4,3,32,1024]{3,2,1,0:T(8,128)} %fs.1, f32[4,32,1024]{2,1,0:T(8,128)} %fk.1, f32[4,32,1024]{2,1,0:T(8,128)} %fr.1, ...), custom_call_target="tpu_custom_call" | custom-call | tf_op jit(solution)/shard_map/pallas_call | solution.py:589
  39.5 0.7 %copy.12 = f32[3,8,16,256]{3,2,1,0:T(8,128)} copy(f32[3,8,16,256]{3,2,1,0:T(8,128)S(1)} %get-tuple-element.2) | data formatting | bytes 786432
  40.2 1.1 %copy.13 = f32[4,3,32,1024]{3,2,1,0:T(8,128)} copy(f32[4,3,32,1024]{3,2,1,0:T(8,128)S(1)} %get-tuple-element.3) | data formatting | bytes 3145728
